TPU v7x, 32 devices: a whole 2x2x4 slice. The times are simulated.
32 devices in a mesh: fsdp: 8 (over y, x, core), seq: 4 (over z).
Axes of the slice: x: 2, y: 2, z: 4, core: 2. Of those that a mesh axis runs over, the one named last changes fastest.
Arguments:
- tokens: bfloat16 [2, 8, 1536, 512], P(None, 'fsdp', 'seq'), may hold values from -6 to 6
- encoded: bfloat16 [2, 8, 256, 512], P(None, 'fsdp', 'seq'), may hold values from -6 to 6
- segment_ids: int32 [2, 8, 1536], P(None, 'fsdp'), may hold values from 0 to 4, as said below
- prefix_len: int32 [2, 8, 4], P(None, 'fsdp'), may hold values from 128 to 512, as said below
- cotangent: bfloat16 [2, 8, 1536, 512], P(None, 'fsdp', 'seq'), may hold values from -6 to 6
- w_query: bfloat16 [512, 512], P('fsdp'), may hold values from -0.25 to 0.25
- w_key: bfloat16 [512, 512], P('fsdp'), may hold values from -0.25 to 0.25
- w_value: bfloat16 [512, 512], P('fsdp'), may hold values from -0.25 to 0.25
- w_out: bfloat16 [512, 512], P('fsdp'), may hold values from -1 to 1
- c_query: bfloat16 [512, 512], P('fsdp'), may hold values from -0.25 to 0.25
- c_key: bfloat16 [512, 512], P('fsdp'), may hold values from -0.25 to 0.25
- c_value: bfloat16 [512, 512], P('fsdp'), may hold values from -0.25 to 0.25
- c_out: bfloat16 [512, 512], P('fsdp'), may hold values from -1 to 1
- w_up: bfloat16 [512, 2048], P('fsdp'), may hold values from -0.25 to 0.25
- b_up: bfloat16 [2048], P('fsdp'), may hold values from -3 to 3
- w_down: bfloat16 [2048, 512], P('fsdp'), may hold values from -0.125 to 0.125
- b_down: bfloat16 [512], P('fsdp'), may hold values from -3 to 3
- gain_one: bfloat16 [512], P('fsdp'), may hold values from 0.099609375 to 1.8984375
- shift_one: bfloat16 [512], P('fsdp'), may hold values from -3 to 3
- gain_two: bfloat16 [512], P('fsdp'), may hold values from 0.099609375 to 1.8984375
- shift_two: bfloat16 [512], P('fsdp'), may hold values from -3 to 3
- gain_three: bfloat16 [512], P('fsdp'), may hold values from 0.099609375 to 1.8984375
- shift_three: bfloat16 [512], P('fsdp'), may hold values from -3 to 3
- w_slot: bfloat16 [1024, 512], P('fsdp'), may hold values from -0.1875 to 0.1875
Outputs:
- slot_out: bfloat16 [2, 8, 1536, 512], P(None, 'fsdp', 'seq')
- grad_tokens: float32 [2, 8, 1536, 512], P(None, 'fsdp', 'seq')
- grad_encoded: float32 [2, 8, 256, 512], P(None, 'fsdp', 'seq')
- grad_w_query: float32 [512, 512], P('fsdp')
- grad_w_key: float32 [512, 512], P('fsdp')
- grad_w_value: float32 [512, 512], P('fsdp')
- grad_w_out: float32 [512, 512], P('fsdp')
- grad_c_query: float32 [512, 512], P('fsdp')
- grad_c_key: float32 [512, 512], P('fsdp')
- grad_c_value: float32 [512, 512], P('fsdp')
- grad_c_out: float32 [512, 512], P('fsdp')
- grad_w_up: float32 [512, 2048], P('fsdp')
- grad_b_up: float32 [2048], P('fsdp')
- grad_w_down: float32 [2048, 512], P('fsdp')
- grad_b_down: float32 [512], P('fsdp')
- grad_gain_one: float32 [512], P('fsdp')
- grad_shift_one: float32 [512], P('fsdp')
- grad_gain_two: float32 [512], P('fsdp')
- grad_shift_two: float32 [512], P('fsdp')
- grad_gain_three: float32 [512], P('fsdp')
- grad_shift_three: float32 [512], P('fsdp')
- grad_w_slot: float32 [1024, 512], P('fsdp')
Inputs may be any that keep to these rules, and one draw needn't show every extreme that they name: `segment_ids`: in every group, positions 0 to 511 hold 0; the later positions hold continuation numbers 1 to 4, never falling, each number present on 128 or more positions. prefix_len[m, g, c] is the number of leading prompt positions that continuation c + 1 sees; continuation 1 of every group sees the whole prompt.
All inputs are finite; a program needn't handle non-finite values.
Results may differ from a plain program's by a relative error of at most 0.024.
Values may be sent and summed in bfloat16 or wider, within the bound.
A program may use at most 128 MiB of HBM per device.

v0:
```python
import math

import jax
import jax.numpy as jnp
from jax import lax
from jax.sharding import PartitionSpec as P

D = 512
HD = 64
MICRO = 2


EPSILON = 1e-05


def passed_along(value, axis, steps):
    count = lax.axis_size(axis)
    first, last = (max(0, -steps), min(count, count - steps))
    return lax.ppermute(value, axis, [(source, source + steps) for source in range(first, last)])


def layer_norm(residual, gain, shift):
    average = jnp.mean(residual, axis=-1, keepdims=True)
    centred = residual - average
    variance = jnp.mean(centred * centred, axis=-1, keepdims=True)
    return centred * lax.rsqrt(variance + EPSILON) * gain + shift


def product(left_side, matrix):
    return jnp.dot(left_side, matrix, preferred_element_type=jnp.float32)


def outer_sum(left_side, right_side):
    return jnp.einsum("lc,ld->cd", left_side, right_side, preferred_element_type=jnp.float32)


def times_back(left_side, matrix):
    return jnp.einsum("ld,cd->lc", left_side, matrix, preferred_element_type=jnp.float32)


def visible(segment, prefix, offset, length):
    own_segment = lax.dynamic_slice_in_dim(segment, offset, length)
    numbers = jnp.arange(1, prefix.shape[0] + 1, dtype=jnp.int32)
    own_prefix = jnp.sum(
        jnp.where(own_segment[:, None] == numbers[None, :], prefix[None, :], 0), axis=1
    )
    places = jnp.arange(segment.shape[0], dtype=jnp.int32)
    same_part = own_segment[:, None] == segment[None, :]
    prompt_part = (segment[None, :] == 0) & (places[None, :] < own_prefix[:, None])
    return same_part | prompt_part


def block_scores(queries, head_keys, segment, prefix, offset, block_size):
    scores = jnp.einsum("qhd,khd->hqk", queries, head_keys, preferred_element_type=jnp.float32) * (
        1.0 / math.sqrt(HD)
    )
    if segment is not None:
        scores = jnp.where(visible(segment, prefix, offset, block_size)[None], scores, -1e30)
    return scores


def attend_forward(query, keys, values, segment, prefix):
    positions = query.shape[0]
    span = keys.shape[0]
    head_count = query.shape[1] // HD
    block_size = min(512, positions)
    head_keys = keys.reshape(span, head_count, HD)
    head_values = values.reshape(span, head_count, HD)

    def one_block(number):
        offset = number * block_size
        queries = lax.dynamic_slice_in_dim(query, offset, block_size, 0).reshape(
            block_size, head_count, HD
        )
        scores = block_scores(queries, head_keys, segment, prefix, offset, block_size)
        maximum = jnp.max(scores, axis=-1, keepdims=True)
        raw_weight = jnp.exp(scores - maximum)
        denom_sum = jnp.sum(raw_weight, axis=-1, keepdims=True)
        attn_prob = raw_weight / denom_sum
        mixture = jnp.einsum(
            "hqk,khd->qhd",
            attn_prob.astype(jnp.bfloat16),
            head_values,
            preferred_element_type=jnp.float32,
        )
        log_total = maximum[..., 0] + jnp.log(denom_sum[..., 0])
        return (mixture.reshape(block_size, head_count * HD).astype(jnp.bfloat16), log_total)

    mixture, log_total = lax.map(one_block, jnp.arange(positions // block_size, dtype=jnp.int32))
    return (mixture.reshape(positions, head_count * HD), log_total)


def attend_backward(query, keys, values, log_total, d_mixture, segment, prefix):
    positions = query.shape[0]
    span = keys.shape[0]
    head_count = query.shape[1] // HD
    block_size = min(512, positions)
    scale = 1.0 / math.sqrt(HD)
    head_keys = keys.reshape(span, head_count, HD)
    head_values = values.reshape(span, head_count, HD)

    def one_block(carry, inputs):
        d_keys, d_values = carry
        number, block_total = inputs
        offset = number * block_size
        queries = lax.dynamic_slice_in_dim(query, offset, block_size, 0).reshape(
            block_size, head_count, HD
        )
        d_rows = lax.dynamic_slice_in_dim(d_mixture, offset, block_size, 0).reshape(
            block_size, head_count, HD
        )
        scores = block_scores(queries, head_keys, segment, prefix, offset, block_size)
        attn_prob = jnp.exp(scores - block_total[..., None])
        d_prob = jnp.einsum("qhd,khd->hqk", d_rows, head_values, preferred_element_type=jnp.float32)
        inner = jnp.sum(attn_prob * d_prob, axis=-1, keepdims=True)
        d_scores = (attn_prob * (d_prob - inner)).astype(jnp.bfloat16)
        d_query = (
            jnp.einsum("hqk,khd->qhd", d_scores, head_keys, preferred_element_type=jnp.float32)
            * scale
        )
        d_keys = (
            d_keys
            + jnp.einsum("hqk,qhd->khd", d_scores, queries, preferred_element_type=jnp.float32)
            * scale
        )
        d_values = d_values + jnp.einsum(
            "hqk,qhd->khd",
            attn_prob.astype(jnp.bfloat16),
            d_rows,
            preferred_element_type=jnp.float32,
        )
        return (
            (d_keys, d_values),
            d_query.reshape(block_size, head_count * HD).astype(jnp.bfloat16),
        )

    zero_rows = jnp.zeros((span, head_count, HD), jnp.float32)
    numbers = jnp.arange(positions // block_size, dtype=jnp.int32)
    (d_keys, d_values), d_query = lax.scan(one_block, (zero_rows, zero_rows), (numbers, log_total))
    d_pair = jnp.stack(
        [d_keys.reshape(span, head_count * HD), d_values.reshape(span, head_count * HD)]
    )
    return (d_query.reshape(positions, head_count * HD), d_pair.astype(jnp.bfloat16))


def on_device(
    tokens,
    encoded,
    segment_ids,
    prefix_len,
    cotangent,
    w_query,
    w_key,
    w_value,
    w_out,
    c_query,
    c_key,
    c_value,
    c_out,
    w_up,
    b_up,
    w_down,
    b_down,
    gain_one,
    shift_one,
    gain_two,
    shift_two,
    gain_three,
    shift_three,
    w_slot,
):
    (
        all_query,
        all_key,
        all_value,
        all_out,
        all_cquery,
        all_ckey,
        all_cvalue,
        all_cout,
        all_up,
        all_upbias,
        all_down,
        all_downbias,
        all_gain_one,
        all_shift_one,
        all_gain_two,
        all_shift_two,
        all_gain_three,
        all_shift_three,
        all_slot,
    ) = (
        lax.all_gather(w_query, "fsdp", axis=0, tiled=True),
        lax.all_gather(w_key, "fsdp", axis=0, tiled=True),
        lax.all_gather(w_value, "fsdp", axis=0, tiled=True),
        lax.all_gather(w_out, "fsdp", axis=0, tiled=True),
        lax.all_gather(c_query, "fsdp", axis=0, tiled=True),
        lax.all_gather(c_key, "fsdp", axis=0, tiled=True),
        lax.all_gather(c_value, "fsdp", axis=0, tiled=True),
        lax.all_gather(c_out, "fsdp", axis=0, tiled=True),
        lax.all_gather(w_up, "fsdp", axis=0, tiled=True),
        lax.all_gather(b_up, "fsdp", axis=0, tiled=True),
        lax.all_gather(w_down, "fsdp", axis=0, tiled=True),
        lax.all_gather(b_down, "fsdp", axis=0, tiled=True),
        lax.all_gather(gain_one, "fsdp", axis=0, tiled=True),
        lax.all_gather(shift_one, "fsdp", axis=0, tiled=True),
        lax.all_gather(gain_two, "fsdp", axis=0, tiled=True),
        lax.all_gather(shift_two, "fsdp", axis=0, tiled=True),
        lax.all_gather(gain_three, "fsdp", axis=0, tiled=True),
        lax.all_gather(shift_three, "fsdp", axis=0, tiled=True),
        lax.all_gather(w_slot, "fsdp", axis=0, tiled=True),
    )
    self_weights = jnp.stack([all_query, all_key, all_value], axis=1)
    cross_weights = jnp.stack([all_ckey, all_cvalue], axis=1)
    up_bias = all_upbias.astype(jnp.float32)
    down_bias = all_downbias.astype(jnp.float32)
    norm_one = (all_gain_one.astype(jnp.float32), all_shift_one.astype(jnp.float32))
    norm_two = (all_gain_two.astype(jnp.float32), all_shift_two.astype(jnp.float32))
    norm_three = (all_gain_three.astype(jnp.float32), all_shift_three.astype(jnp.float32))
    seq_rank = lax.axis_index("seq")
    totals = [
        jnp.zeros(matrix.shape, jnp.float32)
        for matrix in (
            all_query,
            all_key,
            all_value,
            all_out,
            all_cquery,
            all_ckey,
            all_cvalue,
            all_cout,
            all_up,
            all_upbias,
            all_down,
            all_downbias,
            all_gain_one,
            all_shift_one,
            all_gain_two,
            all_shift_two,
            all_gain_three,
            all_shift_three,
            all_slot,
        )
    ]
    slot_list = []
    token_grads = []
    encoded_grads = []
    for micro in range(MICRO):
        tokens_low = tokens[micro, 0]
        tokens_full = tokens_low.astype(jnp.float32)
        encoded_low = encoded[micro, 0]
        segment = segment_ids[micro, 0]
        prefix = prefix_len[micro, 0]
        upstream = cotangent[micro, 0]
        row_count = tokens_low.shape[0]
        qkv_rows = jnp.einsum(
            "ld,dcf->clf", tokens_low, self_weights, preferred_element_type=jnp.float32
        ).astype(jnp.bfloat16)
        encoded_kv = jnp.einsum(
            "ld,dcf->clf", encoded_low, cross_weights, preferred_element_type=jnp.float32
        ).astype(jnp.bfloat16)
        self_heads, encoded_heads = (
            lax.all_to_all(qkv_rows, "seq", split_axis=2, concat_axis=1, tiled=True),
            lax.all_to_all(encoded_kv, "seq", split_axis=2, concat_axis=1, tiled=True),
        )
        mix_heads, self_total = attend_forward(
            self_heads[0], self_heads[1], self_heads[2], segment, prefix
        )
        mix_rows = lax.all_to_all(mix_heads, "seq", split_axis=0, concat_axis=1, tiled=True)
        normed_one, back_one = jax.vjp(
            layer_norm, tokens_full + product(mix_rows, all_out), norm_one[0], norm_one[1]
        )
        normed_one_low = normed_one.astype(jnp.bfloat16)
        cross_query = product(normed_one_low, all_cquery).astype(jnp.bfloat16)
        cross_query_heads = lax.all_to_all(
            cross_query, "seq", split_axis=1, concat_axis=0, tiled=True
        )
        cross_heads_mix, cross_total = attend_forward(
            cross_query_heads, encoded_heads[0], encoded_heads[1], None, None
        )
        cross_rows = lax.all_to_all(cross_heads_mix, "seq", split_axis=0, concat_axis=1, tiled=True)
        normed_two, back_two = jax.vjp(
            layer_norm, normed_one + product(cross_rows, all_cout), norm_two[0], norm_two[1]
        )
        normed_two_low = normed_two.astype(jnp.bfloat16)
        pre_act = product(normed_two_low, all_up) + up_bias
        act_full, act_back = jax.vjp(jax.nn.gelu, pre_act)
        activation = act_full.astype(jnp.bfloat16)
        normed_three, back_three = jax.vjp(
            layer_norm,
            normed_two + product(activation, all_down) + down_bias,
            norm_three[0],
            norm_three[1],
        )
        normed_three_low = normed_three.astype(jnp.bfloat16)
        first_next = passed_along(normed_three_low[:1], "seq", -1)
        offset = seq_rank * row_count
        own_segment = lax.dynamic_slice_in_dim(segment, offset, row_count)
        padded_segment = jnp.concatenate([segment, jnp.full((1,), -1, jnp.int32)])
        after_segment = lax.dynamic_slice_in_dim(padded_segment, offset + 1, row_count)
        follow_mask = (own_segment == after_segment).astype(jnp.bfloat16)[:, None]
        follow = jnp.concatenate([normed_three_low[1:], first_next], axis=0) * follow_mask
        joined = jnp.concatenate([normed_three_low, follow], axis=1)
        slot_list.append(product(joined, all_slot).astype(jnp.bfloat16))
        totals[18] = totals[18] + outer_sum(joined, upstream)
        d_joined = times_back(upstream, all_slot)
        d_follow = d_joined[:, D:].astype(jnp.bfloat16) * follow_mask
        carried = passed_along(d_follow[row_count - 1 :], "seq", 1)
        d_three = d_joined[:, :D] + jnp.concatenate([carried, d_follow[:-1]], axis=0).astype(
            jnp.float32
        )
        d_res_three, d_gain_three, d_shift_three = back_three(d_three)
        totals[16] = totals[16] + d_gain_three
        totals[17] = totals[17] + d_shift_three
        d_ffn = d_res_three.astype(jnp.bfloat16)
        totals[11] = totals[11] + jnp.sum(d_ffn.astype(jnp.float32), axis=0)
        totals[10] = totals[10] + outer_sum(activation, d_ffn)
        d_pre = act_back(times_back(d_ffn, all_down))[0].astype(jnp.bfloat16)
        totals[9] = totals[9] + jnp.sum(d_pre.astype(jnp.float32), axis=0)
        totals[8] = totals[8] + outer_sum(normed_two_low, d_pre)
        d_two = d_res_three + times_back(d_pre, all_up)
        d_res_two, d_gain_two, d_shift_two = back_two(d_two)
        totals[14] = totals[14] + d_gain_two
        totals[15] = totals[15] + d_shift_two
        d_cross = d_res_two.astype(jnp.bfloat16)
        totals[7] = totals[7] + outer_sum(cross_rows, d_cross)
        d_cross_mix = times_back(d_cross, all_cout).astype(jnp.bfloat16)
        d_cross_heads = lax.all_to_all(d_cross_mix, "seq", split_axis=1, concat_axis=0, tiled=True)
        d_cq_heads, d_ckv_heads = attend_backward(
            cross_query_heads,
            encoded_heads[0],
            encoded_heads[1],
            cross_total,
            d_cross_heads,
            None,
            None,
        )
        d_cq_rows, d_ckv_rows = (
            lax.all_to_all(d_cq_heads[None], "seq", split_axis=1, concat_axis=2, tiled=True),
            lax.all_to_all(d_ckv_heads, "seq", split_axis=1, concat_axis=2, tiled=True),
        )
        d_cq = d_cq_rows[0]
        totals[4] = totals[4] + outer_sum(normed_one_low, d_cq)
        totals[5] = totals[5] + outer_sum(encoded_low, d_ckv_rows[0])
        totals[6] = totals[6] + outer_sum(encoded_low, d_ckv_rows[1])
        encoded_grads.append(
            jnp.einsum("clf,dcf->ld", d_ckv_rows, cross_weights, preferred_element_type=jnp.float32)
        )
        d_one = d_res_two + times_back(d_cq, all_cquery)
        d_res_one, d_gain_one, d_shift_one = back_one(d_one)
        totals[12] = totals[12] + d_gain_one
        totals[13] = totals[13] + d_shift_one
        d_attn = d_res_one.astype(jnp.bfloat16)
        totals[3] = totals[3] + outer_sum(mix_rows, d_attn)
        d_self_mix = times_back(d_attn, all_out).astype(jnp.bfloat16)
        d_self_heads = lax.all_to_all(d_self_mix, "seq", split_axis=1, concat_axis=0, tiled=True)
        d_q_heads, d_kv_heads = attend_backward(
            self_heads[0], self_heads[1], self_heads[2], self_total, d_self_heads, segment, prefix
        )
        d_qkv_heads = jnp.concatenate([d_q_heads[None], d_kv_heads], axis=0)
        d_qkv = lax.all_to_all(d_qkv_heads, "seq", split_axis=1, concat_axis=2, tiled=True)
        grad_self = jnp.einsum("ld,clf->dcf", tokens_low, d_qkv, preferred_element_type=jnp.float32)
        totals[0] = totals[0] + grad_self[:, 0]
        totals[1] = totals[1] + grad_self[:, 1]
        totals[2] = totals[2] + grad_self[:, 2]
        token_grads.append(
            d_res_one
            + jnp.einsum("clf,dcf->ld", d_qkv, self_weights, preferred_element_type=jnp.float32)
        )
    (
        sum_query,
        sum_key,
        sum_value,
        sum_out,
        sum_cquery,
        sum_ckey,
        sum_cvalue,
        sum_cout,
        sum_up,
        sum_upbias,
        sum_down,
        sum_downbias,
        sum_gain_one,
        sum_shift_one,
        sum_gain_two,
        sum_shift_two,
        sum_gain_three,
        sum_shift_three,
        sum_slot,
    ) = totals
    (
        sum_query,
        sum_key,
        sum_value,
        sum_out,
        sum_cquery,
        sum_ckey,
        sum_cvalue,
        sum_cout,
        sum_up,
        sum_upbias,
        sum_down,
        sum_downbias,
        sum_gain_one,
        sum_shift_one,
        sum_gain_two,
        sum_shift_two,
        sum_gain_three,
        sum_shift_three,
        sum_slot,
    ) = (
        lax.psum(sum_query.astype(jnp.bfloat16), "seq").astype(jnp.float32),
        lax.psum(sum_key.astype(jnp.bfloat16), "seq").astype(jnp.float32),
        lax.psum(sum_value.astype(jnp.bfloat16), "seq").astype(jnp.float32),
        lax.psum(sum_out.astype(jnp.bfloat16), "seq").astype(jnp.float32),
        lax.psum(sum_cquery.astype(jnp.bfloat16), "seq").astype(jnp.float32),
        lax.psum(sum_ckey.astype(jnp.bfloat16), "seq").astype(jnp.float32),
        lax.psum(sum_cvalue.astype(jnp.bfloat16), "seq").astype(jnp.float32),
        lax.psum(sum_cout.astype(jnp.bfloat16), "seq").astype(jnp.float32),
        lax.psum(sum_up.astype(jnp.bfloat16), "seq").astype(jnp.float32),
        lax.psum(sum_upbias.astype(jnp.bfloat16), "seq").astype(jnp.float32),
        lax.psum(sum_down.astype(jnp.bfloat16), "seq").astype(jnp.float32),
        lax.psum(sum_downbias.astype(jnp.bfloat16), "seq").astype(jnp.float32),
        lax.psum(sum_gain_one.astype(jnp.bfloat16), "seq").astype(jnp.float32),
        lax.psum(sum_shift_one.astype(jnp.bfloat16), "seq").astype(jnp.float32),
        lax.psum(sum_gain_two.astype(jnp.bfloat16), "seq").astype(jnp.float32),
        lax.psum(sum_shift_two.astype(jnp.bfloat16), "seq").astype(jnp.float32),
        lax.psum(sum_gain_three.astype(jnp.bfloat16), "seq").astype(jnp.float32),
        lax.psum(sum_shift_three.astype(jnp.bfloat16), "seq").astype(jnp.float32),
        lax.psum(sum_slot.astype(jnp.bfloat16), "seq").astype(jnp.float32),
    )
    (
        sum_query,
        sum_key,
        sum_value,
        sum_out,
        sum_cquery,
        sum_ckey,
        sum_cvalue,
        sum_cout,
        sum_up,
        sum_upbias,
        sum_down,
        sum_downbias,
        sum_gain_one,
        sum_shift_one,
        sum_gain_two,
        sum_shift_two,
        sum_gain_three,
        sum_shift_three,
        sum_slot,
    ) = (
        lax.psum_scatter(
            sum_query.astype(jnp.bfloat16), "fsdp", scatter_dimension=0, tiled=True
        ).astype(jnp.float32),
        lax.psum_scatter(
            sum_key.astype(jnp.bfloat16), "fsdp", scatter_dimension=0, tiled=True
        ).astype(jnp.float32),
        lax.psum_scatter(
            sum_value.astype(jnp.bfloat16), "fsdp", scatter_dimension=0, tiled=True
        ).astype(jnp.float32),
        lax.psum_scatter(
            sum_out.astype(jnp.bfloat16), "fsdp", scatter_dimension=0, tiled=True
        ).astype(jnp.float32),
        lax.psum_scatter(
            sum_cquery.astype(jnp.bfloat16), "fsdp", scatter_dimension=0, tiled=True
        ).astype(jnp.float32),
        lax.psum_scatter(
            sum_ckey.astype(jnp.bfloat16), "fsdp", scatter_dimension=0, tiled=True
        ).astype(jnp.float32),
        lax.psum_scatter(
            sum_cvalue.astype(jnp.bfloat16), "fsdp", scatter_dimension=0, tiled=True
        ).astype(jnp.float32),
        lax.psum_scatter(
            sum_cout.astype(jnp.bfloat16), "fsdp", scatter_dimension=0, tiled=True
        ).astype(jnp.float32),
        lax.psum_scatter(
            sum_up.astype(jnp.bfloat16), "fsdp", scatter_dimension=0, tiled=True
        ).astype(jnp.float32),
        lax.psum_scatter(
            sum_upbias.astype(jnp.bfloat16), "fsdp", scatter_dimension=0, tiled=True
        ).astype(jnp.float32),
        lax.psum_scatter(
            sum_down.astype(jnp.bfloat16), "fsdp", scatter_dimension=0, tiled=True
        ).astype(jnp.float32),
        lax.psum_scatter(
            sum_downbias.astype(jnp.bfloat16), "fsdp", scatter_dimension=0, tiled=True
        ).astype(jnp.float32),
        lax.psum_scatter(
            sum_gain_one.astype(jnp.bfloat16), "fsdp", scatter_dimension=0, tiled=True
        ).astype(jnp.float32),
        lax.psum_scatter(
            sum_shift_one.astype(jnp.bfloat16), "fsdp", scatter_dimension=0, tiled=True
        ).astype(jnp.float32),
        lax.psum_scatter(
            sum_gain_two.astype(jnp.bfloat16), "fsdp", scatter_dimension=0, tiled=True
        ).astype(jnp.float32),
        lax.psum_scatter(
            sum_shift_two.astype(jnp.bfloat16), "fsdp", scatter_dimension=0, tiled=True
        ).astype(jnp.float32),
        lax.psum_scatter(
            sum_gain_three.astype(jnp.bfloat16), "fsdp", scatter_dimension=0, tiled=True
        ).astype(jnp.float32),
        lax.psum_scatter(
            sum_shift_three.astype(jnp.bfloat16), "fsdp", scatter_dimension=0, tiled=True
        ).astype(jnp.float32),
        lax.psum_scatter(
            sum_slot.astype(jnp.bfloat16), "fsdp", scatter_dimension=0, tiled=True
        ).astype(jnp.float32),
    )
    slot_out = jnp.stack(slot_list)[:, None]
    grad_tokens = jnp.stack(token_grads)[:, None]
    grad_encoded = jnp.stack(encoded_grads)[:, None]
    return (
        slot_out,
        grad_tokens,
        grad_encoded,
        sum_query,
        sum_key,
        sum_value,
        sum_out,
        sum_cquery,
        sum_ckey,
        sum_cvalue,
        sum_cout,
        sum_up,
        sum_upbias,
        sum_down,
        sum_downbias,
        sum_gain_one,
        sum_shift_one,
        sum_gain_two,
        sum_shift_two,
        sum_gain_three,
        sum_shift_three,
        sum_slot,
    )


def solution(mesh):
    in_specs = (
        P(None, "fsdp", "seq", None),
        P(None, "fsdp", "seq", None),
        P(None, "fsdp", None),
        P(None, "fsdp", None),
        P(None, "fsdp", "seq", None),
        P("fsdp", None),
        P("fsdp", None),
        P("fsdp", None),
        P("fsdp", None),
        P("fsdp", None),
        P("fsdp", None),
        P("fsdp", None),
        P("fsdp", None),
        P("fsdp", None),
        P("fsdp"),
        P("fsdp", None),
        P("fsdp"),
        P("fsdp"),
        P("fsdp"),
        P("fsdp"),
        P("fsdp"),
        P("fsdp"),
        P("fsdp"),
        P("fsdp", None),
    )
    out_specs = (
        P(None, "fsdp", "seq", None),
        P(None, "fsdp", "seq", None),
        P(None, "fsdp", "seq", None),
        P("fsdp", None),
        P("fsdp", None),
        P("fsdp", None),
        P("fsdp", None),
        P("fsdp", None),
        P("fsdp", None),
        P("fsdp", None),
        P("fsdp", None),
        P("fsdp", None),
        P("fsdp"),
        P("fsdp", None),
        P("fsdp"),
        P("fsdp"),
        P("fsdp"),
        P("fsdp"),
        P("fsdp"),
        P("fsdp"),
        P("fsdp"),
        P("fsdp", None),
    )
    return jax.shard_map(
        on_device, mesh=mesh, in_specs=in_specs, out_specs=out_specs, check_vma=False
    )
```

profile of v0, /device:TPU:0, one launch (start us, length us, event | category | flops | bytes accessed | tf_op | source)
XLA Modules:
  0.0 1267.3 jit_solution(7657246542687910049)
XLA Ops:
  8.7 11.6 all_gather.64
  57.4 10.0 all_gather.59
  88.9 12.9 %all-reduce.16 = (bf16[512]{0:T(512)(128)(2,1)S(1)}, bf16[512]{0:T(512)(128)(2,1)S(1)}, bf16[512]{0:T(512)(128)(2,1)S(1)}, bf16[512]{0:T(512)(128)(2,1)S(1)}, bf...) all-reduce(bf16[512]{0:T(512)(128)(2,1)S(1)} %dynamic-update-slice.1,, ...), channel_id=1, replica_groups=mesh['fsdp'=8,'seq'=4] {'fsdp'}, use_global_device_ids=true, to_apply=%add.1 | all-reduce | flops 3072 | bytes 12288
  137.0 10.1 all_gather.66
  163.4 26.7 %while.110 = (s32[]{:T(128)}, bf16[3,512,128]{2,1,0:T(8,128)(2,1)}, f32[3,2,512]{2,1,0:T(2,128)S(1)}, s32[3]{0:T(128)S(1)}, s32[1536]{0:T(1024)S(1)}, /*index=5*...) while((s32[]{:T(128)}, bf16[3,512,128]{2,1,0:T(8,128)(2,1)}, ...), condition=%wide.region_19.20_spmd, body=%wide.region_15.19_spmd.sunk | while | flops 424744960 | bytes 23928576 | solution.py:89
  206.5 26.8 %while.108 = (s32[]{:T(128)}, bf16[3,512,128]{2,1,0:T(8,128)(2,1)}, f32[3,2,512]{2,1,0:T(2,128)S(1)}, s32[3]{0:T(128)S(1)}, s32[1536]{0:T(1024)S(1)}, /*index=5*...) while((s32[]{:T(128)}, bf16[3,512,128]{2,1,0:T(8,128)(2,1)}, ...), condition=%wide.region_4.5_spmd, body=%wide.region_0.4_spmd.sunk | while | flops 424744960 | bytes 23928576 | solution.py:89
  272.9 15.0 %while.111 = (s32[]{:T(128)}, bf16[3,512,128]{2,1,0:T(8,128)(2,1)}, f32[3,2,512]{2,1,0:T(2,128)}, s32[3]{0:T(128)}, bf16[1536,128]{0,1:T(8,128)(2,1)S(1)}, /*ind...) while((s32[]{:T(128)}, bf16[3,512,128]{2,1,0:T(8,128)(2,1)}, ...), condition=%wide.region_25.26_spmd, body=%wide.region_22.25_spmd.sunk | while | flops 69008384 | bytes 4359339 | solution.py:89
  297.1 15.7 %while.109 = (s32[]{:T(128)}, bf16[3,512,128]{2,1,0:T(8,128)(2,1)}, f32[3,2,512]{2,1,0:T(2,128)}, s32[3]{0:T(128)S(1)}, bf16[1536,128]{0,1:T(8,128)(2,1)}, /*ind...) while((s32[]{:T(128)}, bf16[3,512,128]{2,1,0:T(8,128)(2,1)}, ...), condition=%wide.region_10.11_spmd, body=%wide.region_7.10_spmd.sunk | while | flops 69008384 | bytes 4359339 | solution.py:89
  390.3 40.9 %while.112 = (s32[]{:T(128)}, f32[256,2,64]{0,2,1:T(8,128)}, f32[256,2,64]{0,2,1:T(8,128)}, bf16[3,512,128]{2,1,0:T(8,128)(2,1)}, s32[3]{0:T(128)}, /*index=5*/b...) while((s32[]{:T(128)}, f32[256,2,64]{0,2,1:T(8,128)}, ...), condition=%wide.region_36.37_spmd.clone, body=%wide.region_34.36_spmd.clone.sunk | while | flops 170163200 | bytes 10572502 | solution.py:139
  439.8 38.9 %while.114 = (s32[]{:T(128)}, f32[256,2,64]{0,2,1:T(8,128)}, f32[256,2,64]{0,2,1:T(8,128)}, bf16[3,512,128]{2,1,0:T(8,128)(2,1)}, s32[3]{0:T(128)S(1)}, /*index=...) while((s32[]{:T(128)}, f32[256,2,64]{0,2,1:T(8,128)}, ...), condition=%wide.region_49.50_spmd.clone, body=%wide.region_47.49_spmd.clone.sunk | while | flops 170163200 | bytes 10572502 | solution.py:139
  571.3 65.9 %while.113 = (s32[]{:T(128)}, f32[1536,2,64]{0,2,1:T(8,128)}, f32[1536,2,64]{0,2,1:T(8,128)}, bf16[3,512,128]{2,1,0:T(8,128)(2,1)}, s32[3]{0:T(128)S(1)}, /*inde...) while((s32[]{:T(128)}, f32[1536,2,64]{0,2,1:T(8,128)}, ...), condition=%wide.region_42.43_spmd.clone, body=%wide.region_39.42_spmd.clone.sunk | while | flops 1025054720 | bytes 87617776 | solution.py:139
  654.6 70.2 %while.115 = (s32[]{:T(128)}, f32[1536,2,64]{0,2,1:T(8,128)}, f32[1536,2,64]{0,2,1:T(8,128)}, bf16[3,512,128]{2,1,0:T(8,128)(2,1)}, s32[3]{0:T(128)S(1)}, /*inde...) while((s32[]{:T(128)}, f32[1536,2,64]{0,2,1:T(8,128)}, ...), condition=%wide.region_55.56_spmd.clone, body=%wide.region_52.55_spmd.clone.sunk | while | flops 1025054720 | bytes 82898848 | solution.py:139
  749.7 13.3 %all-to-all-done.17 = bf16[3,1536,128]{2,0,1:T(4,128)(2,1)} async-done(((bf16[3,1536,128]{2,0,1:T(4,128)(2,1)}), bf16[3,1536,128]{2,0,1:T(4,128)(2,1)}, u32[]{:S(2)}, u32[]{:S(2)}) %all-to-all-start.17) | async-done | bytes 1179680 | tf_op jit(solution)/shard_map/all_to_all | solution.py:361
  781.9 22.4 %all-reduce.15 = (bf16[512]{0:T(512)(128)(2,1)S(1)}, bf16[2048]{0:T(1024)(128)(2,1)}, bf16[512]{0:T(512)(128)(2,1)}, bf16[512]{0:T(512)(128)(2,1)}, bf16[512]{0:...) all-reduce(bf16[512]{0:T(512)(128)(2,1)} %copy-done.198, ...), channel_id=1, replica_groups=mesh['fsdp'=8,'seq'=4] {'fsdp'}, use_global_device_ids=true, to_apply=%add.6 | all-reduce | flops 6144 | bytes 24576
  842.8 10.4 all-reduce.17
  863.5 27.9 %reduce-scatter.36.cloned.1.call-done = bf16[64,512]{1,0:T(8,128)(2,1)} async-done(((bf16[512,512]{1,0:T(8,128)(2,1)}), bf16[64,512]{1,0:T(8,128)(2,1)}) %reduce-scatter.36.cloned.1.call-update) | async-done | bytes 65552
  893.0 36.2 %reduce-scatter.38.cloned.1.call-done = bf16[64,512]{1,0:T(8,128)(2,1)} async-done(((bf16[512,512]{1,0:T(8,128)(2,1)}), bf16[64,512]{1,0:T(8,128)(2,1)}) %reduce-scatter.38.cloned.1.call-update) | async-done | bytes 65552
  930.8 35.9 %reduce-scatter.26.cloned.1.call-done = bf16[64,512]{1,0:T(8,128)(2,1)} async-done(((bf16[512,512]{1,0:T(8,128)(2,1)}), bf16[64,512]{1,0:T(8,128)(2,1)}) %reduce-scatter.26.cloned.1.call-update) | async-done | bytes 65552 | tf_op jit(solution)/shard_map/reduce_scatter | solution.py:474
  966.7 37.1 %reduce-scatter.24.cloned.1.call-done = bf16[64,512]{1,0:T(8,128)(2,1)} async-done(((bf16[512,512]{1,0:T(8,128)(2,1)}), bf16[64,512]{1,0:T(8,128)(2,1)}) %reduce-scatter.24.cloned.1.call-update) | async-done | bytes 65552 | tf_op jit(solution)/shard_map/reduce_scatter | solution.py:465
  1003.8 37.6 %reduce-scatter.22.cloned.1.call-done = bf16[64,512]{1,0:T(8,128)(2,1)} async-done(((bf16[512,512]{1,0:T(8,128)(2,1)}), bf16[64,512]{1,0:T(8,128)(2,1)}) %reduce-scatter.22.cloned.1.call-update) | async-done | bytes 65552 | tf_op jit(solution)/shard_map/reduce_scatter | solution.py:462
  1041.3 39.1 %reduce-scatter.32.cloned.1.call-done = bf16[128,512]{1,0:T(8,128)(2,1)} async-done(((bf16[1024,512]{1,0:T(8,128)(2,1)}), bf16[128,512]{1,0:T(8,128)(2,1)}) %reduce-scatter.32.cloned.1.call-update) | async-done | bytes 131088 | tf_op jit(solution)/shard_map/reduce_scatter | solution.py:507
  1080.4 44.5 %reduce-scatter.30.cloned.1.call-done = bf16[256,512]{1,0:T(8,128)(2,1)} async-done(((bf16[2048,512]{1,0:T(8,128)(2,1)}), bf16[256,512]{1,0:T(8,128)(2,1)}) %reduce-scatter.30.cloned.1.call-update) | async-done | bytes 262160 | tf_op jit(solution)/shard_map/reduce_scatter | solution.py:483
  1125.0 44.8 %reduce-scatter.28.cloned.1.call-done = bf16[64,2048]{1,0:T(8,128)(2,1)} async-done(((bf16[512,2048]{1,0:T(8,128)(2,1)}), bf16[64,2048]{1,0:T(8,128)(2,1)}) %reduce-scatter.28.cloned.1.call-update) | async-done | bytes 262160 | tf_op jit(solution)/shard_map/reduce_scatter | solution.py:477
  1176.1 68.9 %all-reduce.21.cloned.1.call-done = (bf16[64,512]{0,1:T(8,128)(2,1)}, bf16[64,512]{0,1:T(8,128)(2,1)}, bf16[64,512]{0,1:T(8,128)(2,1)}, bf16[64,512]{0,1:T(8,128...) async-done(((bf16[64,512]{0,1:T(8,128)(2,1)}, ...) | async-done | bytes 1179664 | tf_op jit(solution)/shard_map/psum | solution.py:412
  (1207 shorter events, 767.9 us)
Async XLA Ops:
  7.2 226.1 %all-gather.9.cloned.1.call-start = ((), (), s32[]{:S(2)}) async-start(), calls=%async_computation.33 | async-start | bytes 1179648 | tf_op jit(solution)/shard_map/all_gather | solution.py:211
  7.9 331.0 %all-gather.5.cloned.1.call-start = ((), (), s32[]{:S(2)}) async-start(), calls=%async_computation.31 | async-start | bytes 2359296 | tf_op jit(solution)/shard_map/all_gather | solution.py:201
  32.2 37.6 %all-to-all-start.8 = ((bf16[4,2,8192]{2,1,0:T(2,128)(2,1)}), bf16[4,2,8192]{2,1,0:T(2,128)(2,1)S(1)}, u32[]{:S(2)}, u32[]{:S(2)}) async-start(bf16[4,2,8192]{2,1,0:T(2,128)(2,1)} %reshape.926), calls=%async_computation.8 | async-start | bytes 262144 | tf_op jit(solution)/shard_map/all_to_all | solution.py:264
  81.0 70.3 %all-to-all-start.5 = ((bf16[3,384,512]{1,0,2:T(4,128)(2,1)}), bf16[3,384,512]{1,0,2:T(4,128)(2,1)}, u32[]{:S(2)}, u32[]{:S(2)}) async-start(bf16[3,384,512]{1,0,2:T(4,128)(2,1)} %copy.438), calls=%async_computation.5 | async-start | bytes 3145728 | tf_op jit(solution)/shard_map/all_to_all | solution.py:263
  85.4 258.0 %all-gather.7.cloned.1.call-start = ((), (), s32[]{:S(2)}) async-start(), calls=%async_computation.32 | async-start | bytes 2359296 | tf_op jit(solution)/shard_map/all_gather | solution.py:203
  151.3 42.2 %all-to-all-start = ((bf16[3,384,512]{1,0,2:T(4,128)(2,1)}), bf16[3,384,512]{1,0,2:T(4,128)(2,1)}, u32[]{:S(2)}, u32[]{:S(2)}) async-start(bf16[3,384,512]{1,0,2:T(4,128)(2,1)} %copy.424), calls=%async_computation | async-start | bytes 3145728 | tf_op jit(solution)/shard_map/all_to_all | solution.py:263
  193.5 43.1 %all-to-all-start.6 = ((bf16[4,384,128]{2,1,0:T(8,128)(2,1)}), bf16[4,384,128]{2,1,0:T(8,128)(2,1)S(1)}, u32[]{:S(2)}, u32[]{:S(2)}) async-start(bf16[4,384,128]{2,1,0:T(8,128)(2,1)} %bitcast.55), calls=%async_computation.6 | async-start | bytes 786432 | tf_op jit(solution)/shard_map/all_to_all | solution.py:269
  319.3 31.9 %collective-permute-start.2 = (bf16[1,512]{1,0:T(2,128)(2,1)S(1)}, bf16[1,512]{1,0:T(2,128)(2,1)S(1)}, u32[]{:S(2)}, u32[]{:S(2)}) collective-permute-start(bf16[1,512]{1,0:T(2,128)(2,1)S(1)} %slice.210), channel_id=1, source_target_pairs={{0,1},{1,2},{2,3},{4,5},{5,6},{6,7},{8,9},{9,10},{10,11},{12,13},{... | collective-permute-start | bytes 3080 | tf_op jit(solution)/shard_map/ppermute | solution.py:19
  384.8 48.9 %all-to-all-start.14 = ((bf16[384,4,128]{2,0,1:T(8,128)(2,1)}), bf16[384,4,128]{2,0,1:T(8,128)(2,1)}, u32[]{:S(2)}, u32[]{:S(2)}) async-start(bf16[384,4,128]{2,0,1:T(8,128)(2,1)} %bitcast.478), calls=%async_computation.14 | async-start | bytes 786432 | tf_op jit(solution)/shard_map/all_to_all | solution.py:328
  433.8 59.4 %all-to-all-start.18 = ((bf16[2,256,128]{2,0,1:T(2,128)(2,1)}), bf16[2,256,128]{2,0,1:T(2,128)(2,1)}, u32[]{:S(2)}, u32[]{:S(2)}) async-start(bf16[2,256,128]{2,0,1:T(2,128)(2,1)} %copy.486), calls=%async_computation.18 | async-start | bytes 262144 | tf_op jit(solution)/shard_map/all_to_all | solution.py:340
  566.0 82.6 %all-to-all-start.16 = ((bf16[384,4,128]{2,0,1:T(8,128)(2,1)}), bf16[384,4,128]{2,0,1:T(8,128)(2,1)}, u32[]{:S(2)}, u32[]{:S(2)}) async-start(bf16[384,4,128]{2,0,1:T(8,128)(2,1)} %bitcast.477), calls=%async_computation.16 | async-start | bytes 786432 | tf_op jit(solution)/shard_map/all_to_all | solution.py:356
  648.6 87.5 %all-to-all-start.13 = ((bf16[3,1536,128]{2,0,1:T(4,128)(2,1)}), bf16[3,1536,128]{2,0,1:T(4,128)(2,1)}, u32[]{:S(2)}, u32[]{:S(2)}) async-start(bf16[3,1536,128]{2,0,1:T(4,128)(2,1)} %copy.465), calls=%async_computation.13 | async-start | bytes 3145728 | tf_op jit(solution)/shard_map/all_to_all | solution.py:361
  741.2 117.5 %reduce-scatter.42.cloned.1.call-start = ((), (), s32[]{:S(2)}) async-start(), calls=%async_computation.44 | async-start | bytes 589824
  743.0 117.3 %reduce-scatter.40.cloned.1.call-start = ((), (), s32[]{:S(2)}) async-start(), calls=%async_computation.43 | async-start | bytes 589824
  745.0 116.8 %reduce-scatter.34.cloned.1.call-start = ((), (), s32[]{:S(2)}) async-start(), calls=%async_computation.40 | async-start | bytes 589824
  771.5 119.9 %reduce-scatter.36.cloned.1.call-start = ((), (), s32[]{:S(2)}) async-start(), calls=%async_computation.41 | async-start | bytes 589824
  774.5 154.7 %reduce-scatter.38.cloned.1.call-start = ((), (), s32[]{:S(2)}) async-start(), calls=%async_computation.42 | async-start | bytes 589824
  777.8 188.9 %reduce-scatter.26.cloned.1.call-start = ((), (), s32[]{:S(2)}) async-start(), calls=%async_computation.36 | async-start | bytes 589824 | tf_op jit(solution)/shard_map/reduce_scatter | solution.py:474
  780.4 223.4 %reduce-scatter.24.cloned.1.call-start = ((), (), s32[]{:S(2)}) async-start(), calls=%async_computation.35 | async-start | bytes 589824 | tf_op jit(solution)/shard_map/reduce_scatter | solution.py:465
  809.2 232.1 %reduce-scatter.22.cloned.1.call-start = ((), (), s32[]{:S(2)}) async-start(), calls=%async_computation.34 | async-start | bytes 589824 | tf_op jit(solution)/shard_map/reduce_scatter | solution.py:462
  817.4 263.0 %reduce-scatter.32.cloned.1.call-start = ((), (), s32[]{:S(2)}) async-start(), calls=%async_computation.39 | async-start | bytes 1179648 | tf_op jit(solution)/shard_map/reduce_scatter | solution.py:507
  824.2 300.8 %reduce-scatter.30.cloned.1.call-start = ((), (), s32[]{:S(2)}) async-start(), calls=%async_computation.38 | async-start | bytes 2359296 | tf_op jit(solution)/shard_map/reduce_scatter | solution.py:483
  831.1 338.6 %reduce-scatter.28.cloned.1.call-start = ((), (), s32[]{:S(2)}) async-start(), calls=%async_computation.37 | async-start | bytes 2359296 | tf_op jit(solution)/shard_map/reduce_scatter | solution.py:477
  837.2 407.7 %all-reduce.21.cloned.1.call-start = ((), (), s32[]{:S(2)}) async-start(), calls=%async_computation.45 | async-start | bytes 3014656 | tf_op jit(solution)/shard_map/psum | solution.py:412
  (265 other events, 4083.1 us)
Sparse Core Ops, SparseCore 0:
  9.9 26.1 all-gather.8
  38.0 29.0 all-gather.4
  88.1 28.4 all-gather.6
  744.8 34.5 reduce-scatter.41
  782.6 34.1 reduce-scatter.39
  819.7 34.1 reduce-scatter.33
  857.3 34.0 reduce-scatter.35
  895.0 34.1 reduce-scatter.37
  932.6 34.0 reduce-scatter.25
  969.6 34.1 reduce-scatter.23
  1007.2 34.1 reduce-scatter.21
  1044.4 36.0 reduce-scatter.31
  1083.7 41.1 reduce-scatter.29
  1128.4 41.2 reduce-scatter.27
  1174.0 70.8 all-reduce.20
where the time goes:
time: 1280 us; the launch traced here: 1270 us
  waiting for transfers between devices  429 us (34%)
  local copies, waits for them, and re-layouts  243 us (19%)
  matrix products  219 us (17%)
  blocking collectives  134 us (10%)
  starting transfers between devices  103 us (8%)
  other arithmetic  102 us (8%)
  between operations  19.5 us (2%)
  loops' own time  17.2 us (1%)
    psum x1, waiting for transfers between devices, on_device(): lax.psum(sum_query.astype(jnp.bfloat16), 'seq').astype(jnp.float32)  68.9 us
    unnamed x20, waiting for transfers between devices  66.4 us
    unnamed x468, local copies, waits for them, and re-layouts  48 us
    reduce_scatter x1, waiting for transfers between devices, on_device(): lax.psum_scatter(sum_up.astype(jnp.bfloat16), 'fsdp', scatter_dimension=0...  44.8 us
    reduce_scatter x1, waiting for transfers between devices, on_device(): lax.psum_scatter(sum_down.astype(jnp.bfloat16), 'fsdp', scatter_dimension...  44.5 us
    reduce_scatter x1, waiting for transfers between devices, on_device(): lax.psum_scatter(sum_slot.astype(jnp.bfloat16), 'fsdp', scatter_dimension...  39.1 us
    dynamic_update_slice x48, local copies, waits for them, and re-layouts, attend_forward(): lax.map(one_block, jnp.arange(positions // block_size, dtype=jnp.int32))  39 us
    reduce_scatter x1, waiting for transfers between devices, on_device(): lax.psum_scatter(sum_out.astype(jnp.bfloat16), 'fsdp', scatter_dimension=...  37.6 us
  transfers between devices with their start and end apart: 39, of which 19 were waited for; matrix products, arithmetic and copies ran while one was open for 40% of the time, Pallas kernels for 0%

commit v1 on v0

v1 whole, which is shorter than its diff:
```python
import functools
import math

import jax
import jax.numpy as jnp
from jax import lax
from jax.experimental import pallas as pl
from jax.experimental.pallas import tpu as pltpu
from jax.sharding import PartitionSpec as P

D = 512
HD = 64
HEADS = 8
FF = 2048
MICRO = 2
HALO = 16
EPSILON = 1e-05
BF = jnp.bfloat16
F32 = jnp.float32
SCALE = 1.0 / math.sqrt(HD)
NEG = -1e30
MIB = 1024 * 1024
GELU_C = math.sqrt(2.0 / math.pi)

VM = pl.BlockSpec(memory_space=pltpu.VMEM)


def nn(a, b):
    return lax.dot_general(a, b, (((1,), (0,)), ((), ())), preferred_element_type=F32)


def nt(a, b):
    return lax.dot_general(a, b, (((1,), (1,)), ((), ())), preferred_element_type=F32)


def tn(a, b):
    return lax.dot_general(a, b, (((0,), (0,)), ((), ())), preferred_element_type=F32)


def lanes_of(pair):
    return pl.ds(pl.multiple_of(pair * 128, 128), 128)


def head_masked(value, head):
    lane = lax.broadcasted_iota(jnp.int32, value.shape, 1)
    return jnp.where((lane >= 64) == (head == 1), value, jnp.zeros_like(value))


def softmax_parts(scores):
    top = jnp.max(scores, axis=-1, keepdims=True)
    raw = jnp.exp(scores - top)
    total = jnp.sum(raw, axis=-1, keepdims=True)
    return raw, top, total


def attend_pair(query_pair, key_pair, value_pair, bias, pair, lse_ref):
    mixed = []
    for head in range(2):
        scores = nt(head_masked(query_pair, head), key_pair)
        if bias is not None:
            scores = scores + bias
        raw, top, total = softmax_parts(scores)
        mixed.append(nn(raw.astype(BF), value_pair) / total)
        lane = lax.broadcasted_iota(jnp.int32, lse_ref.shape, 1)
        lse_ref[...] = jnp.where(lane == pair * 2 + head, top + jnp.log(total), lse_ref[...])
    lane = lax.broadcasted_iota(jnp.int32, mixed[0].shape, 1)
    return jnp.where(lane < 64, mixed[0], mixed[1])


def self_forward_kernel(
    glen, rows, x_ref, wq_ref, wk_ref, wv_ref, col_ref, row_ref,
    q_ref, k_ref, v_ref, mix_ref, lse_out, bias, lse_sc,
):
    prompt = glen // 3
    rank = lax.axis_index("seq")
    off = pl.multiple_of(rank * rows, 128)
    edge = pl.multiple_of(jnp.minimum(rank * rows + rows, glen - HALO), HALO)
    wk = wk_ref[...].reshape(D, D)
    wv = wv_ref[...].reshape(D, D)
    wq = wq_ref[...].reshape(D, D)

    def project(tile, _):
        at = pl.ds(pl.multiple_of(tile * 256, 256), 256)
        part = x_ref[0, at, :]
        k_ref[0, at, :] = nn(part, wk).astype(BF)
        v_ref[0, at, :] = nn(part, wv).astype(BF)
        return 0

    lax.fori_loop(0, glen // 256, project, 0)
    q_ref[0, 0:rows, :] = (nn(x_ref[0, pl.ds(off, rows), :], wq).astype(BF) * SCALE).astype(BF)
    q_ref[0, rows : rows + HALO, :] = (
        nn(x_ref[0, pl.ds(edge, HALO), :], wq).astype(BF) * SCALE
    ).astype(BF)
    seg_row = row_ref[0, 0:1, :]
    place = lax.broadcasted_iota(jnp.int32, (1, glen), 1)
    for start, count, src in ((0, rows, off), (rows, HALO, edge)):
        info = col_ref[0, pl.ds(src, count), :]
        limit = info[:, 0:1]
        seg = info[:, 1:2]
        seen = jnp.where(place < prompt, (place < limit).astype(jnp.int32), (seg_row == seg).astype(jnp.int32))
        bias[start : start + count, :] = jnp.where(seen == 1, 0.0, NEG)

    def one_pair(pair, _):
        at = lanes_of(pair)
        mix = attend_pair(q_ref[0, :, at], k_ref[0, :, at], v_ref[0, :, at], bias[...], pair, lse_sc)
        mix_ref[0, :, at] = mix.astype(BF)
        return 0

    lax.fori_loop(0, HEADS // 2, one_pair, 0)
    lse_out[0] = lse_sc[0:rows, :].T[0:HEADS, :]


def self_forward(x_all, wq, wk, wv, col, row, rows):
    glen = x_all.shape[1]
    ext = rows + HALO
    n, piece = wq.shape[0], wq.shape[1]
    weight = pl.BlockSpec((n, piece, D), lambda m: (0, 0, 0))

    def micro(*shape):
        return pl.BlockSpec((1,) + shape, lambda m: (m, 0, 0))

    return pl.pallas_call(
        functools.partial(self_forward_kernel, glen, rows),
        grid=(MICRO,),
        in_specs=[micro(glen, D), weight, weight, weight, micro(glen, 2), micro(1, glen)],
        out_specs=[micro(ext, D), micro(glen, D), micro(glen, D), micro(ext, D), micro(HEADS, rows)],
        out_shape=[
            jax.ShapeDtypeStruct((MICRO, ext, D), BF),
            jax.ShapeDtypeStruct((MICRO, glen, D), BF),
            jax.ShapeDtypeStruct((MICRO, glen, D), BF),
            jax.ShapeDtypeStruct((MICRO, ext, D), BF),
            jax.ShapeDtypeStruct((MICRO, HEADS, rows), F32),
        ],
        scratch_shapes=[pltpu.VMEM((ext, glen), F32), pltpu.VMEM((ext, 128), F32)],
        compiler_params=pltpu.CompilerParams(vmem_limit_bytes=56 * MIB),
        name="self_forward",
    )(x_all, wq, wk, wv, col, row)


def norm_forward(residual, gain, shift):
    average = jnp.mean(residual, axis=-1, keepdims=True)
    centred = residual - average
    variance = jnp.mean(centred * centred, axis=-1, keepdims=True)
    rstd = lax.rsqrt(variance + EPSILON)
    hat = centred * rstd
    return hat * gain + shift, hat, rstd


def norm_backward(upstream, hat, rstd, gain):
    d_hat = upstream * gain
    mean_d = jnp.mean(d_hat, axis=-1, keepdims=True)
    mean_dh = jnp.mean(d_hat * hat, axis=-1, keepdims=True)
    d_gain = jnp.sum(upstream * hat, axis=0, keepdims=True)
    d_shift = jnp.sum(upstream, axis=0, keepdims=True)
    return rstd * (d_hat - mean_d - hat * mean_dh), d_gain, d_shift


def gelu_parts(value):
    square = value * value
    t = jnp.tanh(GELU_C * value * (1.0 + 0.044715 * square))
    half = 0.5 * (1.0 + t)
    slope = half + 0.5 * value * (1.0 - t * t) * (GELU_C * (1.0 + 3.0 * 0.044715 * square))
    return value * half, slope


def head_sums(product_rows):
    rows, cols = 16, product_rows.shape[1]
    head = lax.broadcasted_iota(jnp.int32, (rows, cols), 0)
    lane = lax.broadcasted_iota(jnp.int32, (rows, cols), 1)
    pick = ((lane // HD) == head).astype(F32)
    return lax.dot_general(
        pick, product_rows, (((1,), (1,)), ((), ())),
        preferred_element_type=F32, precision=lax.Precision.HIGHEST,
    )[0:HEADS, :]


def middle_kernel(
    rows, enc,
    mix_ref, x_ref, e_ref, cot_ref, shifted_ref, flag_ref,
    wout_ref, cq_ref, ck_ref, cv_ref, cout_ref, up_ref, down_ref, slot_ref,
    bup_ref, vec_ref,
    slot_out, dmix_out, dr1_out, genc_out,
    gout, gcq, gck, gcv, gcout, gup, gdown, gslot, gbup, gvec,
    lowx, lown, cqs, cks, cvs, lse_sc, lse_row, cmix, h1s, hats, rstds, slope,
    act, dpre, dffn, dcross, dcqs, dattn, dcks, dcvs, ckt, h3s, h2low,
):
    ext = rows + HALO
    n = wout_ref.shape[0]
    gbup[...] = jnp.zeros_like(gbup)
    gvec[...] = jnp.zeros_like(gvec)

    def vec(i):
        return vec_ref[i : i + 1, :]

    def one_micro(m, _):
        own = pl.ds(0, rows)
        attn = nn(mix_ref[m], wout_ref[...].reshape(D, D))
        h1, hat, rstd = norm_forward(x_ref[m].astype(F32) + attn, vec(1), vec(2))
        h1s[...] = h1
        dr1_out[m] = hat[0:rows]
        rstds[:, 0:1] = rstd[0:rows]
        h1_low = h1.astype(BF)
        lown[0, m] = h1_low[0:rows]
        cqs[...] = (nn(h1_low, cq_ref[...].reshape(D, D)).astype(BF) * SCALE).astype(BF)
        cks[...] = nn(e_ref[m], ck_ref[...].reshape(D, D)).astype(BF)
        cvs[...] = nn(e_ref[m], cv_ref[...].reshape(D, D)).astype(BF)

        def cross_pair(pair, _):
            at = lanes_of(pair)
            mix = attend_pair(cqs[:, at], cks[:, at], cvs[:, at], None, pair, lse_sc)
            cmix[:, at] = mix.astype(BF)
            return 0

        lax.fori_loop(0, HEADS // 2, cross_pair, 0)
        lse_row[0:HEADS, :] = lse_sc[0:rows, :].T[0:HEADS, :]
        lowx[m] = cmix[0:rows, :]
        h2, hat, rstd = norm_forward(
            h1s[...] + nn(cmix[...], cout_ref[...].reshape(D, D)), vec(3), vec(4)
        )
        h1s[...] = h2
        hats[...] = hat[0:rows]
        rstds[:, 1:2] = rstd[0:rows]
        h2low[...] = h2.astype(BF)
        lown[1, m] = h2low[0:rows, :]
        h3s[...] = jnp.zeros_like(h3s)

        for c in range(FF // D):
            at = slice(c * D, (c + 1) * D)
            pre = nn(h2low[...], up_ref[:, :, at].reshape(D, D)) + bup_ref[0:1, at]
            value, grad = gelu_parts(pre)
            value = value.astype(BF)
            act[m, :, at] = value[0:rows]
            slope[:, at] = grad[0:rows]
            down = down_ref[...].reshape(FF, D)[c * D : (c + 1) * D, :]
            h3s[...] += nn(value, down)
        h3, hat, rstd = norm_forward(h1s[...] + h3s[...] + vec(0), vec(5), vec(6))
        h3_low = h3.astype(BF)
        h3s[...] = h3_low.astype(F32)
        lown[2, m] = h3_low[0:rows]
        top = slot_ref[...].reshape(2 * D, D)[0:D, :]
        bottom = slot_ref[...].reshape(2 * D, D)[D : 2 * D, :]
        flags = flag_ref[m]
        follow = (h3s[pl.ds(1, rows), :] * flags[:, 0:1]).astype(BF)
        slot_out[m] = (nn(h3_low[0:rows], top) + nn(follow, bottom)).astype(BF)
        d_follow = nt(shifted_ref[m], bottom).astype(BF).astype(F32) * flags[:, 1:2]
        d_three = nt(cot_ref[m], top) + d_follow
        d_r3, d_gain, d_shift = norm_backward(d_three, hat[0:rows], rstd[0:rows], vec(5))
        gvec[5:6, :] += d_gain
        gvec[6:7, :] += d_shift
        d_ffn = d_r3.astype(BF)
        dffn[m] = d_ffn
        gvec[0:1, :] += jnp.sum(d_ffn.astype(F32), axis=0, keepdims=True)
        d_two = d_r3
        for c in range(FF // D):
            at = slice(c * D, (c + 1) * D)
            down = down_ref[...].reshape(FF, D)[c * D : (c + 1) * D, :]
            grad = (nt(d_ffn, down) * slope[:, at]).astype(BF)
            dpre[m, :, at] = grad
            gbup[0:1, at] += jnp.sum(grad.astype(F32), axis=0, keepdims=True)
            d_two = d_two + nt(grad, up_ref[:, :, at].reshape(D, D))
        d_r2, d_gain, d_shift = norm_backward(d_two, hats[...], rstds[:, 1:2], vec(3))
        gvec[3:4, :] += d_gain
        gvec[4:5, :] += d_shift
        d_cross = d_r2.astype(BF)
        dcross[m] = d_cross
        d_cmix = nt(d_cross, cout_ref[...].reshape(D, D)).astype(BF)
        dmix_out[m] = d_cmix
        delta = head_sums(d_cmix.astype(F32) * cmix[0:rows, :].astype(F32))
        lse_row[HEADS : 2 * HEADS, :] = delta
        ckt[...] = cks[...].T

        def cross_back(pair, _):
            at = lanes_of(pair)
            kp, vp = cks[:, at], cvs[:, at]
            qp, dp = cqs[0:rows, at], dmix_out[m, :, at]
            kt = ckt[at, :]
            d_k = d_v = None
            d_qt = []
            for head in range(2):
                qm, dm = head_masked(qp, head), head_masked(dp, head)
                row = pair * 2 + head
                prob = jnp.exp(nt(kp, qm) - lse_row[pl.ds(row, 1), :])
                d_score = (prob * (nt(vp, dm) - lse_row[pl.ds(HEADS + row, 1), :])).astype(BF)
                dk, dv = nn(d_score, qm), nn(prob.astype(BF), dm)
                d_k = dk if d_k is None else d_k + dk
                d_v = dv if d_v is None else d_v + dv
                d_qt.append(nn(kt, d_score))
            sub = lax.broadcasted_iota(jnp.int32, d_qt[0].shape, 0)
            d_q = jnp.where(sub < 64, d_qt[0], d_qt[1]) * SCALE
            dcqs[m, :, at] = d_q.T.astype(BF)
            dcks[m, :, at] = d_k.astype(BF)
            dcvs[m, :, at] = d_v.astype(BF)
            return 0

        lax.fori_loop(0, HEADS // 2, cross_back, 0)
        genc_out[m] = (
            nt(dcks[m], ck_ref[...].reshape(D, D)) + nt(dcvs[m], cv_ref[...].reshape(D, D))
        ).astype(BF)
        d_one = d_r2 + nt(dcqs[m], cq_ref[...].reshape(D, D))
        d_r1, d_gain, d_shift = norm_backward(d_one, dr1_out[m], rstds[:, 0:1], vec(1))
        gvec[1:2, :] += d_gain
        gvec[2:3, :] += d_shift
        dr1_out[m] = d_r1
        d_attn = d_r1.astype(BF)
        dattn[m] = d_attn
        dmix_out[m] = nt(d_attn, wout_ref[...].reshape(D, D)).astype(BF)
        return 0

    lax.fori_loop(0, MICRO, one_micro, 0)

    total = MICRO * rows

    def flat(ref, *lead):
        return ref[lead].reshape(total, D) if lead else ref[...].reshape(total, D)

    def grad_of(left, right):
        return tn(left, right).astype(BF)

    cot = cot_ref[...].reshape(total, D)
    flagged = jnp.concatenate(
        [(shifted_ref[m].astype(F32) * flag_ref[m][:, 1:2]).astype(BF) for m in range(MICRO)], axis=0
    )
    h3_all = lown[2].reshape(total, D)
    half = n // 2
    gslot[0:half] = grad_of(h3_all, cot).reshape(half, D // half, D)
    gslot[half:n] = grad_of(h3_all, flagged).reshape(half, D // half, D)
    many = n * D // FF
    dffn_all = dffn[...].reshape(total, D)
    for c in range(FF // D):
        at = slice(c * D, (c + 1) * D)
        gdown[c * many : (c + 1) * many] = grad_of(
            act[:, :, at].reshape(total, D), dffn_all
        ).reshape(many, D // many, D)
        gup[:, :, at] = grad_of(lown[1].reshape(total, D), dpre[:, :, at].reshape(total, D)).reshape(
            n, D // n, D
        )
    gcout[...] = grad_of(lowx[...].reshape(total, D), dcross[...].reshape(total, D)).reshape(gcout.shape)
    gcq[...] = grad_of(lown[0].reshape(total, D), dcqs[...].reshape(total, D)).reshape(gcq.shape)
    e_all = e_ref[...].reshape(MICRO * enc, D)
    gck[...] = grad_of(e_all, dcks[...].reshape(MICRO * enc, D)).reshape(gck.shape)
    gcv[...] = grad_of(e_all, dcvs[...].reshape(MICRO * enc, D)).reshape(gcv.shape)
    mix_all = jnp.concatenate([mix_ref[m, 0:rows, :] for m in range(MICRO)], axis=0)
    gout[...] = grad_of(mix_all, dattn[...].reshape(total, D)).reshape(gout.shape)


def middle(mix, x_ext, e_all, cot, shifted, flags, weights, bup, vecs, rows):
    enc = e_all.shape[1]
    ext = rows + HALO
    wout, cq, ck, cv, cout, up, down, slot = weights

    def like(a):
        return jax.ShapeDtypeStruct(a.shape, BF)

    out_shape = [
        jax.ShapeDtypeStruct((MICRO, rows, D), BF),
        jax.ShapeDtypeStruct((MICRO, rows, D), BF),
        jax.ShapeDtypeStruct((MICRO, rows, D), F32),
        jax.ShapeDtypeStruct((MICRO, enc, D), BF),
        like(wout), like(cq), like(ck), like(cv), like(cout), like(up), like(down), like(slot),
        jax.ShapeDtypeStruct((8, FF), F32),
        jax.ShapeDtypeStruct((8, D), F32),
    ]
    V = pltpu.VMEM
    scratch = [
        V((MICRO, rows, D), BF),
        V((3, MICRO, rows, D), BF),
        V((ext, D), BF), V((enc, D), BF), V((enc, D), BF),
        V((ext, 128), F32), V((2 * HEADS, rows), F32),
        V((ext, D), BF),
        V((ext, D), F32),
        V((rows, D), F32), V((rows, 128), F32),
        V((rows, FF), F32),
        V((MICRO, rows, FF), BF), V((MICRO, rows, FF), BF),
        V((MICRO, rows, D), BF), V((MICRO, rows, D), BF), V((MICRO, rows, D), BF),
        V((MICRO, rows, D), BF),
        V((MICRO, enc, D), BF), V((MICRO, enc, D), BF),
        V((D, enc), BF),
        V((ext, D), F32), V((ext, D), BF),
    ]
    return pl.pallas_call(
        functools.partial(middle_kernel, rows, enc),
        in_specs=[VM] * 16,
        out_specs=[VM] * len(out_shape),
        out_shape=out_shape,
        scratch_shapes=scratch,
        compiler_params=pltpu.CompilerParams(vmem_limit_bytes=60 * MIB),
        name="middle",
    )(mix, x_ext, e_all, cot, shifted, flags, wout, cq, ck, cv, cout, up, down, slot, bup, vecs)


def self_backward_kernel(
    glen, rows,
    x_ref, q_ref, k_ref, v_ref, mix_ref, dmix_ref, dr1_ref, lse_ref, row_ref,
    wq_ref, wk_ref, wv_ref,
    own_out, part_out, gq, gk, gv,
    bias, stats, dqt, dqs, dks, dvs,
):
    prompt = glen // 3
    tile = 256
    rank = lax.axis_index("seq")
    off = pl.multiple_of(rank * rows, 128)

    def one_micro(m, _):
        limit = row_ref[m, 0:1, pl.ds(off, rows)]
        seg = row_ref[m, 1:2, pl.ds(off, rows)]

        def masks(t, _):
            at = pl.ds(pl.multiple_of(t * tile, tile), tile)
            place = lax.broadcasted_iota(jnp.int32, (tile, 1), 0) + t * tile
            key_seg = jnp.broadcast_to(row_ref[m, 1:2, at], (8, tile)).T[:, 0:1]
            seen = jnp.where(
                place < prompt, (place < limit).astype(jnp.int32), (key_seg == seg).astype(jnp.int32)
            )
            bias[at, :] = jnp.where(seen == 1, 0.0, NEG)
            return 0

        lax.fori_loop(0, glen // tile, masks, 0)
        stats[0:HEADS, :] = lse_ref[m]
        stats[HEADS : 2 * HEADS, :] = head_sums(
            dmix_ref[m].astype(F32) * mix_ref[m, 0:rows, :].astype(F32)
        )

        def one_pair(pair, _):
            at = lanes_of(pair)
            qp, dp = q_ref[m, 0:rows, at], dmix_ref[m, :, at]
            qm = [head_masked(qp, h) for h in range(2)]
            dm = [head_masked(dp, h) for h in range(2)]
            dqt[...] = jnp.zeros_like(dqt)

            def one_tile(t, _):
                span = pl.ds(pl.multiple_of(t * tile, tile), tile)
                kp, vp = k_ref[m, span, at], v_ref[m, span, at]
                kt = kp.T
                seen = bias[span, :]
                d_k = d_v = None
                d_q = []
                for h in range(2):
                    row = pair * 2 + h
                    prob = jnp.exp(nt(kp, qm[h]) + seen - stats[pl.ds(row, 1), :])
                    d_score = (prob * (nt(vp, dm[h]) - stats[pl.ds(HEADS + row, 1), :])).astype(BF)
                    dk, dv = nn(d_score, qm[h]), nn(prob.astype(BF), dm[h])
                    d_k = dk if d_k is None else d_k + dk
                    d_v = dv if d_v is None else d_v + dv
                    d_q.append(nn(kt, d_score))
                sub = lax.broadcasted_iota(jnp.int32, d_q[0].shape, 0)
                dqt[...] += jnp.where(sub < 64, d_q[0], d_q[1])
                dks[m, span, at] = d_k.astype(BF)
                dvs[m, span, at] = d_v.astype(BF)
                return 0

            lax.fori_loop(0, glen // tile, one_tile, 0)
            dqs[m, :, at] = (dqt[...] * SCALE).T.astype(BF)
            return 0

        lax.fori_loop(0, HEADS // 2, one_pair, 0)
        own_out[m] = dr1_ref[m] + nt(dqs[m], wq_ref[...].reshape(D, D))

        def spread(t, _):
            span = pl.ds(pl.multiple_of(t * tile, tile), tile)
            part_out[m, span, :] = (
                nt(dks[m, span, :], wk_ref[...].reshape(D, D))
                + nt(dvs[m, span, :], wv_ref[...].reshape(D, D))
            ).astype(BF)
            return 0

        lax.fori_loop(0, glen // tile, spread, 0)
        return 0

    lax.fori_loop(0, MICRO, one_micro, 0)
    x_own = jnp.concatenate([x_ref[m, pl.ds(off, rows), :] for m in range(MICRO)], axis=0)
    gq[...] = tn(x_own, dqs[...].reshape(MICRO * rows, D)).astype(BF).reshape(gq.shape)
    x_all = x_ref[...].reshape(MICRO * glen, D)
    gk[...] = tn(x_all, dks[...].reshape(MICRO * glen, D)).astype(BF).reshape(gk.shape)
    gv[...] = tn(x_all, dvs[...].reshape(MICRO * glen, D)).astype(BF).reshape(gv.shape)


def self_backward(x_all, q, k, v, mix, dmix, dr1, lse, row, wq, wk, wv, rows):
    glen = x_all.shape[1]
    V = pltpu.VMEM

    def like(a):
        return jax.ShapeDtypeStruct(a.shape, BF)

    return pl.pallas_call(
        functools.partial(self_backward_kernel, glen, rows),
        in_specs=[VM] * 12,
        out_specs=[VM] * 5,
        out_shape=[
            jax.ShapeDtypeStruct((MICRO, rows, D), F32),
            jax.ShapeDtypeStruct((MICRO, glen, D), BF),
            like(wq), like(wk), like(wv),
        ],
        scratch_shapes=[
            V((glen, rows), F32), V((2 * HEADS, rows), F32), V((128, rows), F32),
            V((MICRO, rows, D), BF), V((MICRO, glen, D), BF), V((MICRO, glen, D), BF),
        ],
        compiler_params=pltpu.CompilerParams(vmem_limit_bytes=60 * MIB),
        name="self_backward",
    )(x_all, q, k, v, mix, dmix, dr1, lse, row, wq, wk, wv)


def passed_along(value, axis, steps):
    count = lax.axis_size(axis)
    first, last = (max(0, -steps), min(count, count - steps))
    return lax.ppermute(value, axis, [(source, source + steps) for source in range(first, last)])


MATRICES = ("wq", "wk", "wv", "wout", "cq", "ck", "cv", "cout", "up", "down", "slot")


def on_device(
    tokens, encoded, segment_ids, prefix_len, cotangent,
    w_query, w_key, w_value, w_out, c_query, c_key, c_value, c_out,
    w_up, b_up, w_down, b_down,
    gain_one, shift_one, gain_two, shift_two, gain_three, shift_three, w_slot,
):
    n = lax.axis_size("fsdp")
    rank = lax.axis_index("seq")
    tokens = tokens[:, 0]
    rows = tokens.shape[1]
    seg = segment_ids[:, 0]
    glen = seg.shape[1]
    prompt = glen // 3
    prefix = prefix_len[:, 0]
    cot = cotangent[:, 0]

    shards = (w_query, w_key, w_value, w_out, c_query, c_key, c_value, c_out, w_up, w_down, w_slot)
    full = [lax.all_gather(w, "fsdp", axis=0, tiled=False) for w in shards]
    wq, wk, wv, wout, cq, ck, cv, cout, up, down, slot = full
    small = jnp.concatenate(
        [b_up, b_down, gain_one, shift_one, gain_two, shift_two, gain_three, shift_three]
    )
    small_all = lax.all_gather(small, "fsdp", axis=0, tiled=False)
    edge = FF // n
    bup = small_all[:, :edge].reshape(1, FF).astype(F32)
    vecs = small_all[:, edge:].reshape(n, 7, D // n).transpose(1, 0, 2).reshape(7, D).astype(F32)
    vecs = jnp.concatenate([vecs, jnp.zeros((1, D), F32)], axis=0)

    x_all = lax.all_gather(tokens, "seq", axis=1, tiled=True)
    e_all = lax.all_gather(encoded[:, 0], "seq", axis=1, tiled=True)
    previous = passed_along(cot[:, rows - HALO :], "seq", 1)[:, HALO - 1 :]
    shifted = jnp.concatenate([previous, cot[:, : rows - 1]], axis=1)

    numbers = jnp.arange(1, prefix.shape[1] + 1, dtype=jnp.int32)
    limit = jnp.sum(
        jnp.where(seg[:, :, None] == numbers[None, None, :], prefix[:, None, :], 0), axis=2
    )
    limit = jnp.where(seg == 0, prompt, limit)
    col = jnp.stack([limit, seg], axis=2)
    row = jnp.stack([limit, seg], axis=1)
    same = jnp.concatenate(
        [jnp.zeros((MICRO, 1), F32), (seg[:, 1:] == seg[:, :-1]).astype(F32), jnp.zeros((MICRO, 1), F32)],
        axis=1,
    )
    offset = rank * rows
    flags = jnp.stack(
        [
            lax.dynamic_slice_in_dim(same, offset + 1, rows, 1),
            lax.dynamic_slice_in_dim(same, offset, rows, 1),
        ],
        axis=2,
    )
    start = jnp.minimum(offset + rows, glen - HALO)
    x_ext = jnp.concatenate([tokens, lax.dynamic_slice_in_dim(x_all, start, HALO, 1)], axis=1)

    q, k, v, mix, lse = self_forward(x_all, wq, wk, wv, col, row[:, 1:2], rows)
    (
        slot_out, dmix, dr1, genc,
        g_out, g_cq, g_ck, g_cv, g_cout, g_up, g_down, g_slot, g_bup, g_vec,
    ) = middle(mix, x_ext, e_all, cot, shifted, flags, (wout, cq, ck, cv, cout, up, down, slot), bup, vecs, rows)
    own, part, g_q, g_k, g_v = self_backward(
        x_all, q, k, v, mix, dmix, dr1, lse, row, wq, wk, wv, rows
    )

    grad_tokens = own + lax.psum_scatter(part, "seq", scatter_dimension=1, tiled=True).astype(F32)
    grad_encoded = lax.psum_scatter(genc, "seq", scatter_dimension=1, tiled=True).astype(F32)
    grads = (g_q, g_k, g_v, g_out, g_cq, g_ck, g_cv, g_cout, g_up, g_down, g_slot)

    def reduced(g):
        g = lax.psum_scatter(g, "fsdp", scatter_dimension=0, tiled=False)
        return lax.psum(g, "seq").astype(F32)

    (g_q, g_k, g_v, g_out, g_cq, g_ck, g_cv, g_cout, g_up, g_down, g_slot) = [reduced(g) for g in grads]
    packed = jnp.concatenate(
        [
            g_bup[0:1].reshape(n, FF // n),
            g_vec[:7].reshape(7, n, D // n).transpose(1, 0, 2).reshape(n, 7 * (D // n)),
        ],
        axis=1,
    )
    packed = lax.psum(packed, ("fsdp", "seq"))
    mine = lax.dynamic_slice_in_dim(packed, lax.axis_index("fsdp"), 1, 0)[0]
    b_up_g = mine[:edge]
    b_down_g, g1, s1, g2, s2, g3, s3 = [
        mine[edge + i * (D // n) : edge + (i + 1) * (D // n)] for i in range(7)
    ]
    return (
        slot_out[:, None], grad_tokens[:, None], grad_encoded[:, None],
        g_q, g_k, g_v, g_out, g_cq, g_ck, g_cv, g_cout,
        g_up, b_up_g, g_down, b_down_g, g1, s1, g2, s2, g3, s3, g_slot,
    )


def solution(mesh):
    act = P(None, "fsdp", "seq", None)
    ids = P(None, "fsdp", None)
    mat, one = P("fsdp", None), P("fsdp")
    in_specs = (
        (act, act, ids, ids, act) + (mat,) * 9 + (one, mat) + (one,) * 7 + (mat,)
    )
    out_specs = (act, act, act) + (mat,) * 9 + (one, mat) + (one,) * 7 + (mat,)
    return jax.shard_map(
        on_device, mesh=mesh, in_specs=in_specs, out_specs=out_specs, check_vma=False
    )
```

time: 1280 us -> 903 us (0.71)
  matrix products: 219 us -> 0 us
  local copies, waits for them, and re-layouts: 243 us -> 24.5 us
  Pallas kernels: 0 us -> 143 us
  starting transfers between devices: 103 us -> 6.21 us
  waiting for transfers between devices: 429 us -> 518 us
  other arithmetic: 102 us -> 22.5 us
  blocking collectives: 134 us -> 172 us
  loops' own time: 17.2 us -> 0 us
    reduce_scatter x6 -> x13, waiting for transfers between devices: 239 us -> 467 us  [the longest x11 416 us: reduced(): g = lax.psum_scatter(g, 'fsdp', scatter_dimension=0, tiled=False)]
    dot_general x134 -> x0, matrix products: 219 us -> none  [the longest x12 36.9 us: one_block(): jnp.einsum('hqk,qhd->khd', attn_prob.astype(jnp.bfloat16), d_rows, prefer...]
    pallas_call x0 -> x3, Pallas kernels: none -> 143 us  [the longest x1 64.5 us: self_backward(): pl.pallas_call(functools.partial(self_backward_kernel, glen, rows), in_sp...]
    all_to_all x20 -> x0, starting transfers between devices: 92.2 us -> none  [the longest x2 10.4 us: on_device(): lax.all_to_all(d_cq_heads[None], 'seq', split_axis=1, concat_axis=2, tile...]
    unnamed x20 -> x18, waiting for transfers between devices: 66.4 us -> 9.22 us
    all_to_all x20 -> x0, waiting for transfers between devices: 53.7 us -> none  [the longest x2 13.3 us: on_device(): lax.all_to_all(d_qkv_heads, 'seq', split_axis=1, concat_axis=2, tiled=True)]
    dynamic_slice x86 -> x1, local copies, waits for them, and re-layouts: 44.9 us -> 0.82 us  [on_device(): lax.dynamic_slice_in_dim(x_all, start, HALO, 1)]
    unnamed x468 -> x61, local copies, waits for them, and re-layouts: 48 us -> 4.82 us
  transfers between devices with their start and end apart: 39 -> 19, of which waited for: 19 -> 13; matrix products, arithmetic and copies ran while one was open for 40% -> 5% of each run, Pallas kernels for 0% -> 4%
where the time goes in v1:
time: 903 us; the launch traced here: 901 us
  waiting for transfers between devices  518 us (57%)
  blocking collectives  172 us (19%)
  Pallas kernels  143 us (16%)
  local copies, waits for them, and re-layouts  24.5 us (3%)
  other arithmetic  22.5 us (2%)
  between operations  15.2 us (2%)
    reduce_scatter x11, waiting for transfers between devices, reduced(): g = lax.psum_scatter(g, 'fsdp', scatter_dimension=0, tiled=False)  416 us
    all_gather x8, blocking collectives, on_device(): full = [lax.all_gather(w, 'fsdp', axis=0, tiled=False) for w in shards]  89.3 us
    pallas_call x1, Pallas kernels, self_backward(): pl.pallas_call(functools.partial(self_backward_kernel, glen, rows), in_sp...  64.5 us
    reduce_scatter x1, waiting for transfers between devices, on_device(): lax.psum_scatter(part, 'seq', scatter_dimension=1, tiled=True).astype(F32)  51.2 us
    pallas_call x1, Pallas kernels, middle(): pl.pallas_call(functools.partial(middle_kernel, rows, enc), in_specs=[VM]...  45.7 us
    psum x1, waiting for transfers between devices, reduced(): return lax.psum(g, 'seq').astype(F32)  41.8 us
    psum x1, blocking collectives, on_device(): packed = lax.psum(packed, ('fsdp', 'seq'))  39.9 us
    pallas_call x1, Pallas kernels, self_forward(): pl.pallas_call(functools.partial(self_forward_kernel, glen, rows), grid=(...  32.9 us
  transfers between devices with their start and end apart: 19, of which 13 were waited for; matrix products, arithmetic and copies ran while one was open for 5% of the time, Pallas kernels for 4%

profile of v1, /device:TPU:0, one launch (start us, length us, event | category | flops | bytes accessed | tf_op | source)
XLA Modules:
  0.0 901.2 jit_solution(992358299497974870)
XLA Ops:
  29.7 25.4 %all-reduce.1 = bf16[5632]{0:T(1024)(128)(2,1)} all-reduce(bf16[5632]{0:T(1024)(128)(2,1)} %dynamic-update-slice), channel_id=15, replica_groups=mesh['fsdp'=8,'seq'=4] {'fsdp'}, use_global_device_ids=true, to_apply=%add.1 | all-reduce | flops 5632 | bytes 22528
  61.8 11.2 %all-gather.1 = bf16[512,512]{1,0:T(8,128)(2,1)} all-gather(bf16[64,512]{1,0:T(8,128)(2,1)} %param.29), channel_id=3, replica_groups=mesh['fsdp'=8,'seq'=4] {'fsdp'}, dimensions={0}, use_global_device_ids=true | all-gather | bytes 589824 | tf_op jit(solution)/shard_map/all_gather | solution.py:528
  73.1 11.1 %all-gather.2 = bf16[512,512]{1,0:T(8,128)(2,1)} all-gather(bf16[64,512]{1,0:T(8,128)(2,1)} %param.30), channel_id=4, replica_groups=mesh['fsdp'=8,'seq'=4] {'fsdp'}, dimensions={0}, use_global_device_ids=true | all-gather | bytes 589824 | tf_op jit(solution)/shard_map/all_gather | solution.py:528
  106.0 11.1 %all-gather.6 = bf16[512,512]{1,0:T(8,128)(2,1)} all-gather(bf16[64,512]{1,0:T(8,128)(2,1)S(1)} %copy-done.10), channel_id=8, replica_groups=mesh['fsdp'=8,'seq'=4] {'fsdp'}, dimensions={0}, use_global_device_ids=true | all-gather | bytes 589824 | tf_op jit(solution)/shard_map/all_gather | solution.py:528
  117.1 12.6 %all-gather.7 = bf16[512,512]{1,0:T(8,128)(2,1)} all-gather(bf16[64,512]{1,0:T(8,128)(2,1)S(1)} %copy-done.11), channel_id=9, replica_groups=mesh['fsdp'=8,'seq'=4] {'fsdp'}, dimensions={0}, use_global_device_ids=true | all-gather | bytes 589824 | tf_op jit(solution)/shard_map/all_gather | solution.py:528
  140.0 11.2 %all-gather.9 = bf16[512,512]{1,0:T(8,128)(2,1)} all-gather(bf16[64,512]{1,0:T(8,128)(2,1)S(1)} %copy-done.13), channel_id=11, replica_groups=mesh['fsdp'=8,'seq'=4] {'fsdp'}, dimensions={0}, use_global_device_ids=true | all-gather | bytes 589824 | tf_op jit(solution)/shard_map/all_gather | solution.py:528
  152.1 17.2 %all-gather.4 = bf16[2,1,256,512]{3,2,0,1:T(8,128)(2,1)} all-gather(bf16[2,1,64,512]{3,2,0,1:T(8,128)(2,1)S(1)} %bitcast.104), channel_id=6, replica_groups=mesh['fsdp'=8,'seq'=4] {'seq'}, dimensions={2}, use_global_device_ids=true | all-gather | bytes 655360 | tf_op jit(solution)/shard_map/all_gather | solution.py:540
  176.5 32.9 %self_forward.1 = (bf16[2,400,512]{2,1,0:T(8,128)(2,1)}, bf16[2,1536,512]{2,1,0:T(8,128)(2,1)}, bf16[2,1536,512]{2,1,0:T(8,128)(2,1)}, bf16[2,400,512]{2,1,0:T(8,128)(2,1)}, f32[2,8,384]{2,1,0:T(8,128)}) custom-call(bf16[2,1536,512]{2,1,0:T(8,128)(2,1)} %bitcast.78, bf16[8,64,512]{2,1,0:T(8,128)(2,1)} %bitcast.80, bf16[8,64,512]{2,1,0:T(8,128)(2,1)} %bitcast.82, ...), custom_call_target="tpu_custom_call" | custom-call | tf_op jit(solution)/shard_map/self_forward/pallas_call | solution.py:122
  211.2 45.7 %middle.1 = (bf16[2,384,512]{2,1,0:T(8,128)(2,1)}, bf16[2,384,512]{2,1,0:T(8,128)(2,1)}, f32[2,384,512]{2,1,0:T(8,128)}, bf16[2,256,512]{2,1,0:T(8,128)(2,1)}, b...) custom-call(bf16[2,400,512]{2,1,0:T(8,128)(2,1)} %get-tuple-element., ...), custom_call_target="tpu_custom_call" | custom-call | tf_op jit(solution)/shard_map/middle/pallas_call | solution.py:380
  256.9 64.5 %self_backward.1 = (f32[2,384,512]{2,1,0:T(8,128)}, bf16[2,1536,512]{2,1,0:T(8,128)(2,1)}, bf16[8,64,512]{2,1,0:T(8,128)(2,1)}, bf16[8,64,512]{2,1,0:T(8,128)(2,1)}, bf16[8,64,512]{2,1,0:T(8,128)(2,1)}) custom-call(bf16[2,1536,512]{2,1,0:T(8,128)(2,1)} %bitcast.79, bf16[2,400,512]{2,1,0:T(8,128)(2,1)} %get-tuple-element.48.q_ref, ...), custom_call_target="tpu_custom_call" | custom-call | tf_op jit(solution)/shard_map/self_backward/pallas_call | solution.py:484
  328.6 25.2 %reduce-scatter.18.cloned.1.call-done = bf16[1,64,512]{2,1,0:T(8,128)(2,1)} async-done(((bf16[8,64,512]{2,1,0:T(8,128)(2,1)}), bf16[1,64,512]{2,1,0:T(8,128)(2,1)}) %reduce-scatter.18.cloned.1.call-update) | async-done | bytes 65552 | tf_op jit(solution)/shard_map/reduce_scatter | solution.py:580
  353.8 37.4 %reduce-scatter.20.cloned.1.call-done = bf16[1,64,512]{2,1,0:T(8,128)(2,1)} async-done(((bf16[8,64,512]{2,1,0:T(8,128)(2,1)}), bf16[1,64,512]{2,1,0:T(8,128)(2,1)}) %reduce-scatter.20.cloned.1.call-update) | async-done | bytes 65552 | tf_op jit(solution)/shard_map/reduce_scatter | solution.py:580
  391.2 37.3 %reduce-scatter.22.cloned.1.call-done = bf16[1,64,512]{2,1,0:T(8,128)(2,1)} async-done(((bf16[8,64,512]{2,1,0:T(8,128)(2,1)}), bf16[1,64,512]{2,1,0:T(8,128)(2,1)}) %reduce-scatter.22.cloned.1.call-update) | async-done | bytes 65552 | tf_op jit(solution)/shard_map/reduce_scatter | solution.py:580
  428.5 38.1 %reduce-scatter.24.cloned.1.call-done = bf16[1,64,512]{2,1,0:T(8,128)(2,1)} async-done(((bf16[8,64,512]{2,1,0:T(8,128)(2,1)}), bf16[1,64,512]{2,1,0:T(8,128)(2,1)}) %reduce-scatter.24.cloned.1.call-update) | async-done | bytes 65552 | tf_op jit(solution)/shard_map/reduce_scatter | solution.py:580
  466.6 37.3 %reduce-scatter.26.cloned.1.call-done = bf16[1,64,512]{2,1,0:T(8,128)(2,1)} async-done(((bf16[8,64,512]{2,1,0:T(8,128)(2,1)}), bf16[1,64,512]{2,1,0:T(8,128)(2,1)}) %reduce-scatter.26.cloned.1.call-update) | async-done | bytes 65552 | tf_op jit(solution)/shard_map/reduce_scatter | solution.py:580
  503.9 37.4 %reduce-scatter.28.cloned.1.call-done = bf16[1,64,512]{2,1,0:T(8,128)(2,1)} async-done(((bf16[8,64,512]{2,1,0:T(8,128)(2,1)}), bf16[1,64,512]{2,1,0:T(8,128)(2,1)}) %reduce-scatter.28.cloned.1.call-update) | async-done | bytes 65552 | tf_op jit(solution)/shard_map/reduce_scatter | solution.py:580
  541.2 37.3 %reduce-scatter.30.cloned.1.call-done = bf16[1,64,512]{2,1,0:T(8,128)(2,1)} async-done(((bf16[8,64,512]{2,1,0:T(8,128)(2,1)}), bf16[1,64,512]{2,1,0:T(8,128)(2,1)}) %reduce-scatter.30.cloned.1.call-update) | async-done | bytes 65552 | tf_op jit(solution)/shard_map/reduce_scatter | solution.py:580
  578.5 37.4 %reduce-scatter.32.cloned.1.call-done = bf16[1,64,512]{2,1,0:T(8,128)(2,1)} async-done(((bf16[8,64,512]{2,1,0:T(8,128)(2,1)}), bf16[1,64,512]{2,1,0:T(8,128)(2,1)}) %reduce-scatter.32.cloned.1.call-update) | async-done | bytes 65552 | tf_op jit(solution)/shard_map/reduce_scatter | solution.py:580
  615.9 39.2 %reduce-scatter.38.cloned.1.call-done = bf16[1,128,512]{2,1,0:T(8,128)(2,1)} async-done(((bf16[8,128,512]{2,1,0:T(8,128)(2,1)}), bf16[1,128,512]{2,1,0:T(8,128)(2,1)}) %reduce-scatter.38.cloned.1.call-update) | async-done | bytes 131088 | tf_op jit(solution)/shard_map/reduce_scatter | solution.py:580
  655.1 44.4 %reduce-scatter.34.cloned.1.call-done = bf16[1,64,2048]{2,1,0:T(8,128)(2,1)} async-done(((bf16[8,64,2048]{2,1,0:T(8,128)(2,1)}), bf16[1,64,2048]{2,1,0:T(8,128)(2,1)}) %reduce-scatter.34.cloned.1.call-update) | async-done | bytes 262160 | tf_op jit(solution)/shard_map/reduce_scatter | solution.py:580
  699.5 44.8 %reduce-scatter.36.cloned.1.call-done = bf16[1,256,512]{2,1,0:T(8,128)(2,1)} async-done(((bf16[8,256,512]{2,1,0:T(8,128)(2,1)}), bf16[1,256,512]{2,1,0:T(8,128)(2,1)}) %reduce-scatter.36.cloned.1.call-update) | async-done | bytes 262160 | tf_op jit(solution)/shard_map/reduce_scatter | solution.py:580
  746.1 39.9 %psum.93 = f32[8,704]{1,0:T(8,128)S(1)} all-reduce(f32[8,704]{1,0:T(8,128)S(1)} %pad_maximum_fusion.3), channel_id=1, replica_groups=mesh['fsdp'=8,'seq'=4] {'fsdp','seq'}, use_global_device_ids=true, to_apply=%region_21.22 | all-reduce | flops 5632 | bytes 45056 | tf_op jit(solution)/shard_map/psum | solution.py:591
  788.8 41.8 %all-reduce.5.cloned.1.call-done = (bf16[64,512]{1,0:T(8,128)(2,1)}, bf16[64,512]{1,0:T(8,128)(2,1)}, bf16[64,512]{1,0:T(8,128)(2,1)}, bf16[64,512]{1,0:T(8,128)...) async-done(((bf16[64,512]{1,0:T(8,128)(2,1)}, ...) | async-done | bytes 1179664 | tf_op jit(solution)/shard_map/psum | solution.py:581
  840.6 51.2 %reduce-scatter.14.cloned.1.call-done = bf16[2,384,512]{2,1,0:T(8,128)(2,1)} async-done(((bf16[2,1536,512]{2,1,0:T(8,128)(2,1)}), bf16[2,384,512]{2,1,0:T(8,128)(2,1)}) %reduce-scatter.14.cloned.1.call-update) | async-done | bytes 786448 | tf_op jit(solution)/shard_map/reduce_scatter | solution.py:575
  (156 shorter events, 94.6 us)
Async XLA Ops:
  7.2 169.3 %all-gather.19.cloned.1.call-start = ((), (), s32[]{:S(2)}) async-start(), calls=%async_computation.26 | async-start | bytes 3932160 | tf_op jit(solution)/shard_map/all_gather | solution.py:539
  7.9 203.3 %all-gather.25.cloned.1.call-start = ((), (), s32[]{:S(2)}) async-start(), calls=%async_computation.29 | async-start | bytes 1179648 | tf_op jit(solution)/shard_map/all_gather | solution.py:528
  8.7 202.5 %all-gather.21.cloned.1.call-start = ((), (), s32[]{:S(2)}) async-start(), calls=%async_computation.27 | async-start | bytes 2359296 | tf_op jit(solution)/shard_map/all_gather | solution.py:528
  9.4 201.8 %all-gather.23.cloned.1.call-start = ((), (), s32[]{:S(2)}) async-start(), calls=%async_computation.28 | async-start | bytes 2359296 | tf_op jit(solution)/shard_map/all_gather | solution.py:528
  10.9 163.8 %collective-permute-start = (bf16[2,16,512]{2,1,0:T(8,128)(2,1)}, bf16[2,16,512]{2,1,0:T(8,128)(2,1)}, u32[]{:S(2)}, u32[]{:S(2)}) collective-permute-start(bf16[2,16,512]{2,1,0:T(8,128)(2,1)} %slice.100), channel_id=1, source_target_pairs={{0,1},{1,2},{2,3},{4,5},{5,6},{6,7},{8,9},{9,10},{10,11},{12,13},{... | collective-permute-start | bytes 98312 | tf_op jit(solution)/shard_map/ppermute | solution.py:505
  16.4 337.4 %reduce-scatter.18.cloned.1.call-start = ((), (), s32[]{:S(2)}) async-start(), calls=%async_computation.15 | async-start | bytes 589824 | tf_op jit(solution)/shard_map/reduce_scatter | solution.py:580
  61.8 55.2 %copy-start.11 = (bf16[64,512]{1,0:T(8,128)(2,1)S(1)}, bf16[64,512]{1,0:T(8,128)(2,1)}, u32[]{:S(2)}) copy-start(bf16[64,512]{1,0:T(8,128)(2,1)} %param.34) | copy-start | bytes 196612
  73.1 56.6 %copy-start.12 = (bf16[64,512]{1,0:T(8,128)(2,1)S(1)}, bf16[64,512]{1,0:T(8,128)(2,1)}, u32[]{:S(2)}) copy-start(bf16[64,512]{1,0:T(8,128)(2,1)} %param.35) | copy-start | bytes 196612
  84.1 55.9 %copy-start.13 = (bf16[64,512]{1,0:T(8,128)(2,1)S(1)}, bf16[64,512]{1,0:T(8,128)(2,1)}, u32[]{:S(2)}) copy-start(bf16[64,512]{1,0:T(8,128)(2,1)} %param.36) | copy-start | bytes 196612
  95.0 56.2 %copy-start.2 = (f32[2,384,1]{2,1,0:T(8,128)S(1)}, f32[2,384,1]{2,1,0:T(8,128)}, u32[]{:S(2)}) copy-start(f32[2,384,1]{2,1,0:T(8,128)} %copy.113) | copy-start | bytes 9220
  321.4 69.8 %reduce-scatter.20.cloned.1.call-start = ((), (), s32[]{:S(2)}) async-start(), calls=%async_computation.16 | async-start | bytes 589824 | tf_op jit(solution)/shard_map/reduce_scatter | solution.py:580
  322.0 106.5 %reduce-scatter.22.cloned.1.call-start = ((), (), s32[]{:S(2)}) async-start(), calls=%async_computation.17 | async-start | bytes 589824 | tf_op jit(solution)/shard_map/reduce_scatter | solution.py:580
  322.7 143.9 %reduce-scatter.24.cloned.1.call-start = ((), (), s32[]{:S(2)}) async-start(), calls=%async_computation.18 | async-start | bytes 589824 | tf_op jit(solution)/shard_map/reduce_scatter | solution.py:580
  323.5 180.4 %reduce-scatter.26.cloned.1.call-start = ((), (), s32[]{:S(2)}) async-start(), calls=%async_computation.19 | async-start | bytes 589824 | tf_op jit(solution)/shard_map/reduce_scatter | solution.py:580
  324.2 217.0 %reduce-scatter.28.cloned.1.call-start = ((), (), s32[]{:S(2)}) async-start(), calls=%async_computation.20 | async-start | bytes 589824 | tf_op jit(solution)/shard_map/reduce_scatter | solution.py:580
  324.8 253.7 %reduce-scatter.30.cloned.1.call-start = ((), (), s32[]{:S(2)}) async-start(), calls=%async_computation.21 | async-start | bytes 589824 | tf_op jit(solution)/shard_map/reduce_scatter | solution.py:580
  325.5 290.4 %reduce-scatter.32.cloned.1.call-start = ((), (), s32[]{:S(2)}) async-start(), calls=%async_computation.22 | async-start | bytes 589824 | tf_op jit(solution)/shard_map/reduce_scatter | solution.py:580
  326.1 329.0 %reduce-scatter.38.cloned.1.call-start = ((), (), s32[]{:S(2)}) async-start(), calls=%async_computation.25 | async-start | bytes 1179648 | tf_op jit(solution)/shard_map/reduce_scatter | solution.py:580
  326.9 372.7 %reduce-scatter.34.cloned.1.call-start = ((), (), s32[]{:S(2)}) async-start(), calls=%async_computation.23 | async-start | bytes 2359296 | tf_op jit(solution)/shard_map/reduce_scatter | solution.py:580
  327.4 416.8 %reduce-scatter.36.cloned.1.call-start = ((), (), s32[]{:S(2)}) async-start(), calls=%async_computation.24 | async-start | bytes 2359296 | tf_op jit(solution)/shard_map/reduce_scatter | solution.py:580
  328.0 459.2 %reduce-scatter.16.cloned.1.call-start = ((), (), s32[]{:S(2)}) async-start(), calls=%async_computation.14 | async-start | bytes 655360 | tf_op jit(solution)/shard_map/reduce_scatter | solution.py:576
  328.6 502.0 %all-reduce.5.cloned.1.call-start = ((), (), s32[]{:S(2)}) async-start(), calls=%async_computation.30 | async-start | bytes 2359296 | tf_op jit(solution)/shard_map/psum | solution.py:581
  744.3 147.5 %reduce-scatter.14.cloned.1.call-start = ((), (), s32[]{:S(2)}) async-start(), calls=%async_computation.13 | async-start | bytes 3932160 | tf_op jit(solution)/shard_map/reduce_scatter | solution.py:575
  832.6 59.2 %copy-start.3 = (f32[2,384,512]{2,1,0:T(8,128)S(1)}, f32[2,384,512]{2,1,0:T(8,128)}, u32[]{:S(2)}) copy-start(f32[2,384,512]{2,1,0:T(8,128)} %get-tuple-element.54) | copy-start | bytes 4718596
  (23 other events, 320.7 us)
Sparse Core Ops, SparseCore 0:
  9.6 66.1 all-gather.18
  77.7 22.8 all-gather.24
  102.5 30.1 all-gather.20
  134.4 28.5 all-gather.22
  321.5 32.2 reduce-scatter.17
  357.1 34.1 reduce-scatter.19
  394.3 34.1 reduce-scatter.21
  432.4 34.1 reduce-scatter.23
  469.7 34.1 reduce-scatter.25
  507.1 34.1 reduce-scatter.27
  544.3 34.1 reduce-scatter.29
  581.7 34.1 reduce-scatter.31
  619.1 36.0 reduce-scatter.37
  658.3 41.1 reduce-scatter.33
  703.0 41.2 reduce-scatter.35
  747.0 21.6 reduce-scatter.15
  771.9 58.6 all-reduce.4
  832.8 58.9 reduce-scatter.13

commit v2 on v1

--- a/solution.py
+++ b/solution.py
@@ -67,17 +67,96 @@
     return jnp.where(lane < 64, mixed[0], mixed[1])
 
 
+def bit_count(n):
+    return n.bit_length() - 1
+
+
+def qkv_rows(n):
+    piece = D // n
+    return {"wq": (0, piece), "wk": (piece, piece), "wv": (2 * piece, piece)}, 3 * piece
+
+
+def rest_rows(n):
+    piece = D // n
+    table, start = {}, 0
+    for name, times in (
+        ("wout", 1), ("cq", 1), ("ck", 1), ("cv", 1), ("cout", 1), ("up", 4), ("down", 4), ("slot", 2)
+    ):
+        table[name] = (start, times * piece)
+        start += times * piece
+    return table, start
+
+
+def square(ref, table, name):
+    start, count = table[name]
+    return ref[:, start : start + count, :].reshape(D, D)
+
+
+def up_part(ref, table, c):
+    start, count = table["up"]
+    piece = count // 4
+    return ref[:, start + c * piece : start + (c + 1) * piece, :].reshape(D, D)
+
+
+def row_part(ref, table, name, c):
+    start, count = table[name]
+    many = D // count
+    return ref[c * many : (c + 1) * many, start : start + count, :].reshape(D, D)
+
+
+def store_square(ref, table, name, value):
+    start, count = table[name]
+    ref[:, start : start + count, :] = value.reshape(ref.shape[0], count, D)
+
+
+def store_up(ref, table, c, value):
+    start, count = table["up"]
+    piece = count // 4
+    ref[:, start + c * piece : start + (c + 1) * piece, :] = value.reshape(ref.shape[0], piece, D)
+
+
+def store_part(ref, table, name, c, value):
+    start, count = table[name]
+    many = D // count
+    ref[c * many : (c + 1) * many, start : start + count, :] = value.reshape(many, count, D)
+
+
+def my_place(n):
+    me = lax.axis_index("fsdp")
+    bits = [(me // (1 << b)) % 2 for b in range(bit_count(n))]
+    return me, bits
+
+
+def partner_of(me, bits, b):
+    return me + (1 - 2 * bits[b]) * (1 << b)
+
+
+def orders(n):
+    d = bit_count(n)
+    far = list(range(1, d))
+    return [far + [0], far[::-1] + [0]]
+
+
+def at_bits(bits, free, fixed=None):
+    fixed = fixed or {}
+    return tuple(
+        slice(None) if b in free else fixed.get(b, bits[b]) for b in range(len(bits) - 1, -1, -1)
+    )
+
+
+MESH_ID = pl.DeviceIdType.MESH
+
+
 def self_forward_kernel(
-    glen, rows, x_ref, wq_ref, wk_ref, wv_ref, col_ref, row_ref,
+    glen, rows, x_ref, w_ref, col_ref, row_ref,
     q_ref, k_ref, v_ref, mix_ref, lse_out, bias, lse_sc,
 ):
     prompt = glen // 3
     rank = lax.axis_index("seq")
     off = pl.multiple_of(rank * rows, 128)
     edge = pl.multiple_of(jnp.minimum(rank * rows + rows, glen - HALO), HALO)
-    wk = wk_ref[...].reshape(D, D)
-    wv = wv_ref[...].reshape(D, D)
-    wq = wq_ref[...].reshape(D, D)
+    table, _ = qkv_rows(w_ref.shape[0])
+    wq, wk, wv = [square(w_ref, table, name) for name in ("wq", "wk", "wv")]
 
     def project(tile, _):
         at = pl.ds(pl.multiple_of(tile * 256, 256), 256)
@@ -110,11 +189,10 @@
     lse_out[0] = lse_sc[0:rows, :].T[0:HEADS, :]
 
 
-def self_forward(x_all, wq, wk, wv, col, row, rows):
+def self_forward(x_all, w, col, row, rows):
     glen = x_all.shape[1]
     ext = rows + HALO
-    n, piece = wq.shape[0], wq.shape[1]
-    weight = pl.BlockSpec((n, piece, D), lambda m: (0, 0, 0))
+    weight = pl.BlockSpec(w.shape, lambda m: (0, 0, 0))
 
     def micro(*shape):
         return pl.BlockSpec((1,) + shape, lambda m: (m, 0, 0))
@@ -122,7 +200,7 @@
     return pl.pallas_call(
         functools.partial(self_forward_kernel, glen, rows),
         grid=(MICRO,),
-        in_specs=[micro(glen, D), weight, weight, weight, micro(glen, 2), micro(1, glen)],
+        in_specs=[micro(glen, D), weight, micro(glen, 2), micro(1, glen)],
         out_specs=[micro(ext, D), micro(glen, D), micro(glen, D), micro(ext, D), micro(HEADS, rows)],
         out_shape=[
             jax.ShapeDtypeStruct((MICRO, ext, D), BF),
@@ -134,7 +212,7 @@
         scratch_shapes=[pltpu.VMEM((ext, glen), F32), pltpu.VMEM((ext, 128), F32)],
         compiler_params=pltpu.CompilerParams(vmem_limit_bytes=56 * MIB),
         name="self_forward",
-    )(x_all, wq, wk, wv, col, row)
+    )(x_all, w, col, row)
 
 
 def norm_forward(residual, gain, shift):
@@ -177,15 +255,13 @@
 def middle_kernel(
     rows, enc,
     mix_ref, x_ref, e_ref, cot_ref, shifted_ref, flag_ref,
-    wout_ref, cq_ref, ck_ref, cv_ref, cout_ref, up_ref, down_ref, slot_ref,
-    bup_ref, vec_ref,
-    slot_out, dmix_out, dr1_out, genc_out,
-    gout, gcq, gck, gcv, gcout, gup, gdown, gslot, gbup, gvec,
+    w_ref, bup_ref, vec_ref,
+    slot_out, dmix_out, dr1_out, genc_out, g_ref, gbup, gvec,
     lowx, lown, cqs, cks, cvs, lse_sc, lse_row, cmix, h1s, hats, rstds, slope,
     act, dpre, dffn, dcross, dcqs, dattn, dcks, dcvs, ckt, h3s, h2low,
 ):
     ext = rows + HALO
-    n = wout_ref.shape[0]
+    table, _ = rest_rows(w_ref.shape[0])
     gbup[...] = jnp.zeros_like(gbup)
     gvec[...] = jnp.zeros_like(gvec)
 
@@ -194,16 +270,16 @@
 
     def one_micro(m, _):
         own = pl.ds(0, rows)
-        attn = nn(mix_ref[m], wout_ref[...].reshape(D, D))
+        attn = nn(mix_ref[m], square(w_ref, table, "wout"))
         h1, hat, rstd = norm_forward(x_ref[m].astype(F32) + attn, vec(1), vec(2))
         h1s[...] = h1
         dr1_out[m] = hat[0:rows]
         rstds[:, 0:1] = rstd[0:rows]
         h1_low = h1.astype(BF)
         lown[0, m] = h1_low[0:rows]
-        cqs[...] = (nn(h1_low, cq_ref[...].reshape(D, D)).astype(BF) * SCALE).astype(BF)
-        cks[...] = nn(e_ref[m], ck_ref[...].reshape(D, D)).astype(BF)
-        cvs[...] = nn(e_ref[m], cv_ref[...].reshape(D, D)).astype(BF)
+        cqs[...] = (nn(h1_low, square(w_ref, table, "cq")).astype(BF) * SCALE).astype(BF)
+        cks[...] = nn(e_ref[m], square(w_ref, table, "ck")).astype(BF)
+        cvs[...] = nn(e_ref[m], square(w_ref, table, "cv")).astype(BF)
 
         def cross_pair(pair, _):
             at = lanes_of(pair)
@@ -215,7 +291,7 @@
         lse_row[0:HEADS, :] = lse_sc[0:rows, :].T[0:HEADS, :]
         lowx[m] = cmix[0:rows, :]
         h2, hat, rstd = norm_forward(
-            h1s[...] + nn(cmix[...], cout_ref[...].reshape(D, D)), vec(3), vec(4)
+            h1s[...] + nn(cmix[...], square(w_ref, table, "cout")), vec(3), vec(4)
         )
         h1s[...] = h2
         hats[...] = hat[0:rows]
@@ -226,19 +302,19 @@
 
         for c in range(FF // D):
             at = slice(c * D, (c + 1) * D)
-            pre = nn(h2low[...], up_ref[:, :, at].reshape(D, D)) + bup_ref[0:1, at]
+            pre = nn(h2low[...], up_part(w_ref, table, c)) + bup_ref[0:1, at]
             value, grad = gelu_parts(pre)
             value = value.astype(BF)
             act[m, :, at] = value[0:rows]
             slope[:, at] = grad[0:rows]
-            down = down_ref[...].reshape(FF, D)[c * D : (c + 1) * D, :]
+            down = row_part(w_ref, table, "down", c)
             h3s[...] += nn(value, down)
         h3, hat, rstd = norm_forward(h1s[...] + h3s[...] + vec(0), vec(5), vec(6))
         h3_low = h3.astype(BF)
         h3s[...] = h3_low.astype(F32)
         lown[2, m] = h3_low[0:rows]
-        top = slot_ref[...].reshape(2 * D, D)[0:D, :]
-        bottom = slot_ref[...].reshape(2 * D, D)[D : 2 * D, :]
+        top = row_part(w_ref, table, "slot", 0)
+        bottom = row_part(w_ref, table, "slot", 1)
         flags = flag_ref[m]
         follow = (h3s[pl.ds(1, rows), :] * flags[:, 0:1]).astype(BF)
         slot_out[m] = (nn(h3_low[0:rows], top) + nn(follow, bottom)).astype(BF)
@@ -253,17 +329,17 @@
         d_two = d_r3
         for c in range(FF // D):
             at = slice(c * D, (c + 1) * D)
-            down = down_ref[...].reshape(FF, D)[c * D : (c + 1) * D, :]
+            down = row_part(w_ref, table, "down", c)
             grad = (nt(d_ffn, down) * slope[:, at]).astype(BF)
             dpre[m, :, at] = grad
             gbup[0:1, at] += jnp.sum(grad.astype(F32), axis=0, keepdims=True)
-            d_two = d_two + nt(grad, up_ref[:, :, at].reshape(D, D))
+            d_two = d_two + nt(grad, up_part(w_ref, table, c))
         d_r2, d_gain, d_shift = norm_backward(d_two, hats[...], rstds[:, 1:2], vec(3))
         gvec[3:4, :] += d_gain
         gvec[4:5, :] += d_shift
         d_cross = d_r2.astype(BF)
         dcross[m] = d_cross
-        d_cmix = nt(d_cross, cout_ref[...].reshape(D, D)).astype(BF)
+        d_cmix = nt(d_cross, square(w_ref, table, "cout")).astype(BF)
         dmix_out[m] = d_cmix
         delta = head_sums(d_cmix.astype(F32) * cmix[0:rows, :].astype(F32))
         lse_row[HEADS : 2 * HEADS, :] = delta
@@ -294,16 +370,16 @@
 
         lax.fori_loop(0, HEADS // 2, cross_back, 0)
         genc_out[m] = (
-            nt(dcks[m], ck_ref[...].reshape(D, D)) + nt(dcvs[m], cv_ref[...].reshape(D, D))
+            nt(dcks[m], square(w_ref, table, "ck")) + nt(dcvs[m], square(w_ref, table, "cv"))
         ).astype(BF)
-        d_one = d_r2 + nt(dcqs[m], cq_ref[...].reshape(D, D))
+        d_one = d_r2 + nt(dcqs[m], square(w_ref, table, "cq"))
         d_r1, d_gain, d_shift = norm_backward(d_one, dr1_out[m], rstds[:, 0:1], vec(1))
         gvec[1:2, :] += d_gain
         gvec[2:3, :] += d_shift
         dr1_out[m] = d_r1
         d_attn = d_r1.astype(BF)
         dattn[m] = d_attn
-        dmix_out[m] = nt(d_attn, wout_ref[...].reshape(D, D)).astype(BF)
+        dmix_out[m] = nt(d_attn, square(w_ref, table, "wout")).astype(BF)
         return 0
 
     lax.fori_loop(0, MICRO, one_micro, 0)
@@ -321,42 +397,32 @@
         [(shifted_ref[m].astype(F32) * flag_ref[m][:, 1:2]).astype(BF) for m in range(MICRO)], axis=0
     )
     h3_all = lown[2].reshape(total, D)
-    half = n // 2
-    gslot[0:half] = grad_of(h3_all, cot).reshape(half, D // half, D)
-    gslot[half:n] = grad_of(h3_all, flagged).reshape(half, D // half, D)
-    many = n * D // FF
+    store_part(g_ref, table, "slot", 0, grad_of(h3_all, cot))
+    store_part(g_ref, table, "slot", 1, grad_of(h3_all, flagged))
     dffn_all = dffn[...].reshape(total, D)
+    h2_all = lown[1].reshape(total, D)
     for c in range(FF // D):
         at = slice(c * D, (c + 1) * D)
-        gdown[c * many : (c + 1) * many] = grad_of(
-            act[:, :, at].reshape(total, D), dffn_all
-        ).reshape(many, D // many, D)
-        gup[:, :, at] = grad_of(lown[1].reshape(total, D), dpre[:, :, at].reshape(total, D)).reshape(
-            n, D // n, D
-        )
-    gcout[...] = grad_of(lowx[...].reshape(total, D), dcross[...].reshape(total, D)).reshape(gcout.shape)
-    gcq[...] = grad_of(lown[0].reshape(total, D), dcqs[...].reshape(total, D)).reshape(gcq.shape)
+        store_part(g_ref, table, "down", c, grad_of(act[:, :, at].reshape(total, D), dffn_all))
+        store_up(g_ref, table, c, grad_of(h2_all, dpre[:, :, at].reshape(total, D)))
+    store_square(g_ref, table, "cout", grad_of(lowx[...].reshape(total, D), dcross[...].reshape(total, D)))
+    store_square(g_ref, table, "cq", grad_of(lown[0].reshape(total, D), dcqs[...].reshape(total, D)))
     e_all = e_ref[...].reshape(MICRO * enc, D)
-    gck[...] = grad_of(e_all, dcks[...].reshape(MICRO * enc, D)).reshape(gck.shape)
-    gcv[...] = grad_of(e_all, dcvs[...].reshape(MICRO * enc, D)).reshape(gcv.shape)
+    store_square(g_ref, table, "ck", grad_of(e_all, dcks[...].reshape(MICRO * enc, D)))
+    store_square(g_ref, table, "cv", grad_of(e_all, dcvs[...].reshape(MICRO * enc, D)))
     mix_all = jnp.concatenate([mix_ref[m, 0:rows, :] for m in range(MICRO)], axis=0)
-    gout[...] = grad_of(mix_all, dattn[...].reshape(total, D)).reshape(gout.shape)
-
-
-def middle(mix, x_ext, e_all, cot, shifted, flags, weights, bup, vecs, rows):
+    store_square(g_ref, table, "wout", grad_of(mix_all, dattn[...].reshape(total, D)))
+
+
+def middle(mix, x_ext, e_all, cot, shifted, flags, w, bup, vecs, rows):
     enc = e_all.shape[1]
     ext = rows + HALO
-    wout, cq, ck, cv, cout, up, down, slot = weights
-
-    def like(a):
-        return jax.ShapeDtypeStruct(a.shape, BF)
-
     out_shape = [
         jax.ShapeDtypeStruct((MICRO, rows, D), BF),
         jax.ShapeDtypeStruct((MICRO, rows, D), BF),
         jax.ShapeDtypeStruct((MICRO, rows, D), F32),
         jax.ShapeDtypeStruct((MICRO, enc, D), BF),
-        like(wout), like(cq), like(ck), like(cv), like(cout), like(up), like(down), like(slot),
+        jax.ShapeDtypeStruct(w.shape, BF),
         jax.ShapeDtypeStruct((8, FF), F32),
         jax.ShapeDtypeStruct((8, D), F32),
     ]
@@ -379,24 +445,24 @@
     ]
     return pl.pallas_call(
         functools.partial(middle_kernel, rows, enc),
-        in_specs=[VM] * 16,
+        in_specs=[VM] * 9,
         out_specs=[VM] * len(out_shape),
         out_shape=out_shape,
         scratch_shapes=scratch,
         compiler_params=pltpu.CompilerParams(vmem_limit_bytes=60 * MIB),
         name="middle",
-    )(mix, x_ext, e_all, cot, shifted, flags, wout, cq, ck, cv, cout, up, down, slot, bup, vecs)
+    )(mix, x_ext, e_all, cot, shifted, flags, w, bup, vecs)
 
 
 def self_backward_kernel(
     glen, rows,
     x_ref, q_ref, k_ref, v_ref, mix_ref, dmix_ref, dr1_ref, lse_ref, row_ref,
-    wq_ref, wk_ref, wv_ref,
-    own_out, part_out, gq, gk, gv,
+    w_ref, own_out, part_out, g_ref,
     bias, stats, dqt, dqs, dks, dvs,
 ):
     prompt = glen // 3
     tile = 256
+    table, _ = qkv_rows(w_ref.shape[0])
     rank = lax.axis_index("seq")
     off = pl.multiple_of(rank * rows, 128)
 
@@ -453,13 +519,13 @@
             return 0
 
         lax.fori_loop(0, HEADS // 2, one_pair, 0)
-        own_out[m] = dr1_ref[m] + nt(dqs[m], wq_ref[...].reshape(D, D))
+        own_out[m] = dr1_ref[m] + nt(dqs[m], square(w_ref, table, "wq"))
 
         def spread(t, _):
             span = pl.ds(pl.multiple_of(t * tile, tile), tile)
             part_out[m, span, :] = (
-                nt(dks[m, span, :], wk_ref[...].reshape(D, D))
-                + nt(dvs[m, span, :], wv_ref[...].reshape(D, D))
+                nt(dks[m, span, :], square(w_ref, table, "wk"))
+                + nt(dvs[m, span, :], square(w_ref, table, "wv"))
             ).astype(BF)
             return 0
 
@@ -468,27 +534,23 @@
 
     lax.fori_loop(0, MICRO, one_micro, 0)
     x_own = jnp.concatenate([x_ref[m, pl.ds(off, rows), :] for m in range(MICRO)], axis=0)
-    gq[...] = tn(x_own, dqs[...].reshape(MICRO * rows, D)).astype(BF).reshape(gq.shape)
+    store_square(g_ref, table, "wq", tn(x_own, dqs[...].reshape(MICRO * rows, D)).astype(BF))
     x_all = x_ref[...].reshape(MICRO * glen, D)
-    gk[...] = tn(x_all, dks[...].reshape(MICRO * glen, D)).astype(BF).reshape(gk.shape)
-    gv[...] = tn(x_all, dvs[...].reshape(MICRO * glen, D)).astype(BF).reshape(gv.shape)
-
-
-def self_backward(x_all, q, k, v, mix, dmix, dr1, lse, row, wq, wk, wv, rows):
+    store_square(g_ref, table, "wk", tn(x_all, dks[...].reshape(MICRO * glen, D)).astype(BF))
+    store_square(g_ref, table, "wv", tn(x_all, dvs[...].reshape(MICRO * glen, D)).astype(BF))
+
+
+def self_backward(x_all, q, k, v, mix, dmix, dr1, lse, row, w, rows):
     glen = x_all.shape[1]
     V = pltpu.VMEM
-
-    def like(a):
-        return jax.ShapeDtypeStruct(a.shape, BF)
-
     return pl.pallas_call(
         functools.partial(self_backward_kernel, glen, rows),
-        in_specs=[VM] * 12,
-        out_specs=[VM] * 5,
+        in_specs=[VM] * 10,
+        out_specs=[VM] * 3,
         out_shape=[
             jax.ShapeDtypeStruct((MICRO, rows, D), F32),
             jax.ShapeDtypeStruct((MICRO, glen, D), BF),
-            like(wq), like(wk), like(wv),
+            jax.ShapeDtypeStruct(w.shape, BF),
         ],
         scratch_shapes=[
             V((glen, rows), F32), V((2 * HEADS, rows), F32), V((128, rows), F32),
@@ -496,16 +558,494 @@
         ],
         compiler_params=pltpu.CompilerParams(vmem_limit_bytes=60 * MIB),
         name="self_backward",
-    )(x_all, q, k, v, mix, dmix, dr1, lse, row, wq, wk, wv)
-
-
-def passed_along(value, axis, steps):
-    count = lax.axis_size(axis)
-    first, last = (max(0, -steps), min(count, count - steps))
-    return lax.ppermute(value, axis, [(source, source + steps) for source in range(first, last)])
-
-
-MATRICES = ("wq", "wk", "wv", "wout", "cq", "ck", "cv", "cout", "up", "down", "slot")
+    )(x_all, q, k, v, mix, dmix, dr1, lse, row, w)
+
+
+class Chain:
+    def __init__(self, ref, rows, sems, lane, rank, count):
+        self.ref, self.rows, self.lane = ref, rows, lane
+        self.send, self.recv = sems
+        self.rank, self.count = rank, count
+
+    def copy(self, side, step, block, target):
+        at = pl.ds(pl.multiple_of(block * self.rows, 16), self.rows)
+        part = self.ref.at[:, at] if len(self.ref.shape) == 3 else self.ref.at[at]
+        return pltpu.make_async_remote_copy(
+            src_ref=part, dst_ref=part,
+            send_sem=self.send.at[self.lane, side, step], recv_sem=self.recv.at[self.lane, side, step],
+            device_id={"seq": target}, device_id_type=MESH_ID,
+        )
+
+    def start(self, step):
+        r, last = self.rank, self.count - 1
+
+        @pl.when((r < last) & (r - step >= 0))
+        def _():
+            self.copy(0, step, r - step, r + 1).start()
+
+        @pl.when((r > 0) & (r + step <= last))
+        def _():
+            self.copy(1, step, r + step, r - 1).start()
+
+    def arrived(self, step):
+        r, last = self.rank, self.count - 1
+
+        @pl.when(r - 1 - step >= 0)
+        def _():
+            self.copy(0, step, r - 1 - step, r - 1).wait_recv()
+
+        @pl.when(r + 1 + step <= last)
+        def _():
+            self.copy(1, step, r + 1 + step, r + 1).wait_recv()
+
+    def sent(self, step):
+        r, last = self.rank, self.count - 1
+
+        @pl.when((r < last) & (r - step >= 0))
+        def _():
+            self.copy(0, step, r - step, r + 1).wait_send()
+
+        @pl.when((r > 0) & (r + step <= last))
+        def _():
+            self.copy(1, step, r + step, r - 1).wait_send()
+
+
+def weight_units(n):
+    piece = D // n
+    units = []
+    for array, start, count in (
+        (0, 0, 3 * piece), (1, 0, 5 * piece), (1, 5 * piece, 4 * piece),
+        (1, 9 * piece, 4 * piece), (1, 13 * piece, 2 * piece),
+    ):
+        for half in range(2):
+            units.append((array, start, count, half * 256, 256, half))
+    return units
+
+
+def greet(peers):
+    barrier = pltpu.get_barrier_semaphore()
+    for axis, target, when in peers:
+        if when is None:
+            pl.semaphore_signal(barrier, inc=1, device_id={axis: target}, device_id_type=MESH_ID)
+        else:
+
+            @pl.when(when)
+            def _():
+                pl.semaphore_signal(barrier, inc=1, device_id={axis: target}, device_id_type=MESH_ID)
+
+    always = sum(1 for peer in peers if peer[2] is None)
+    amount = jnp.int32(always)
+    for axis, target, when in peers:
+        if when is not None:
+            amount = amount + when.astype(jnp.int32)
+    pl.semaphore_wait(barrier, amount if always < len(peers) else always)
+
+
+def gather_kernel(n, count, rows, erows, *refs):
+    shards = refs[0:11]
+    small, tok, enc, cot = refs[11:15]
+    wa, wb, small_all, x_all, e_all, prev = refs[15:21]
+    local, fsend, frecv, zsend, zrecv, csend, crecv = refs[21:]
+    me, bits = my_place(n)
+    rank = lax.axis_index("seq")
+    last = count - 1
+    piece = D // n
+    d = bit_count(n)
+
+    here = at_bits(bits, ())
+    table_a, _ = qkv_rows(n)
+    table_b, _ = rest_rows(n)
+    copies = []
+
+    def keep(src, dst):
+        copy = pltpu.make_async_copy(src, dst, local.at[len(copies)])
+        copy.start()
+        copies.append(copy)
+
+    keep(tok, x_all.at[:, pl.ds(pl.multiple_of(rank * rows, 16), rows)])
+    keep(enc, e_all.at[:, pl.ds(pl.multiple_of(rank * erows, 16), erows)])
+    names = ("wq", "wk", "wv", "wout", "cq", "ck", "cv", "cout", "up", "down", "slot")
+    for name, shard in zip(names, shards):
+        table, target = (table_a, wa) if name in table_a else (table_b, wb)
+        start, size = table[name]
+        if name == "up":
+            for c in range(4):
+                keep(
+                    shard.at[:, pl.ds(c * D, D)],
+                    target.at[here + (pl.ds(start + c * piece, piece), slice(None))],
+                )
+        else:
+            keep(shard, target.at[here + (pl.ds(start, size), slice(None))])
+    keep(small, small_all.at[here])
+
+    peers = [("fsdp", partner_of(me, bits, b), None) for b in range(d)]
+    peers += [("seq", rank - 1, rank > 0), ("seq", rank + 1, rank < last)]
+    greet(peers)
+
+    arrays = (wa, wb, small_all)
+    units = weight_units(n) + [(2, 0, 8, 0, 128, 0)]
+    order_list = orders(n)
+
+    def hop(u, phase):
+        array, r0, nr, c0, nc, which = units[u]
+        order = order_list[which]
+        b = order[phase]
+        part = arrays[array].at[at_bits(bits, order[:phase]) + (pl.ds(r0, nr), pl.ds(c0, nc))]
+        return pltpu.make_async_remote_copy(
+            src_ref=part, dst_ref=part, send_sem=fsend.at[u, phase], recv_sem=frecv.at[u, phase],
+            device_id={"fsdp": partner_of(me, bits, b)}, device_id_type=MESH_ID,
+        )
+
+    def landed(u, phase):
+        array, r0, nr, c0, nc, which = units[u]
+        order = order_list[which]
+        b = order[phase]
+        part = arrays[array].at[
+            at_bits(bits, order[:phase], {b: 1 - bits[b]}) + (pl.ds(r0, nr), pl.ds(c0, nc))
+        ]
+        pltpu.make_async_remote_copy(
+            src_ref=part, dst_ref=part, send_sem=fsend.at[u, phase], recv_sem=frecv.at[u, phase],
+            device_id={"fsdp": partner_of(me, bits, b)}, device_id_type=MESH_ID,
+        ).wait_recv()
+
+    copies[0].wait()
+    copies[1].wait()
+    chains = [
+        Chain(x_all.at[0], rows, (zsend, zrecv), 0, rank, count),
+        Chain(e_all, erows, (zsend, zrecv), 1, rank, count),
+        Chain(x_all.at[1], rows, (zsend, zrecv), 2, rank, count),
+    ]
+    for chain in chains:
+        chain.start(0)
+    halo = pltpu.make_async_remote_copy(
+        src_ref=cot.at[:, pl.ds(rows - HALO, HALO)], dst_ref=prev, send_sem=csend, recv_sem=crecv,
+        device_id={"seq": rank + 1}, device_id_type=MESH_ID,
+    )
+
+    @pl.when(rank < last)
+    def _():
+        halo.start()
+
+    for copy in copies[2:]:
+        copy.wait()
+    for u in range(len(units)):
+        hop(u, 0).start()
+    jobs = []
+    for phase in range(1, d):
+        for u in range(len(units)):
+            jobs.append((u, phase))
+    steps = [(s, c) for s in range(1, count) for c in chains]
+    share = -(-len(jobs) // max(1, len(steps)))
+    while jobs or steps:
+        for u, phase in jobs[:share]:
+            landed(u, phase - 1)
+            hop(u, phase).start()
+        jobs = jobs[share:]
+        if steps:
+            s, chain = steps.pop(0)
+            chain.arrived(s - 1)
+            if s < count - 1:
+                chain.start(s)
+    for u in range(len(units)):
+        landed(u, d - 1)
+
+    first = pltpu.make_async_copy(cot.at[:, pl.ds(rows - HALO, HALO)], prev, local.at[len(copies)])
+
+    @pl.when(rank > 0)
+    def _():
+        halo.wait_recv()
+
+    @pl.when(rank == 0)
+    def _():
+        first.start()
+        first.wait()
+
+    @pl.when(rank < last)
+    def _():
+        halo.wait_send()
+
+    for u in range(len(units)):
+        for phase in range(d):
+            hop(u, phase).wait_send()
+    for chain in chains:
+        for s in range(count - 1):
+            chain.sent(s)
+
+
+def gather(n, count, shards, small, tok, enc, cot):
+    rows, erows = tok.shape[1], enc.shape[1]
+    lead = (2,) * bit_count(n)
+    _, ra = qkv_rows(n)
+    _, rb = rest_rows(n)
+    units = len(weight_units(n)) + 1
+    d = bit_count(n)
+    hbm = pl.BlockSpec(memory_space=pl.ANY)
+    dma = pltpu.SemaphoreType.DMA
+    return pl.pallas_call(
+        functools.partial(gather_kernel, n, count, rows, erows),
+        in_specs=[hbm] * 15,
+        out_specs=[hbm] * 6,
+        out_shape=[
+            jax.ShapeDtypeStruct(lead + (ra, D), BF),
+            jax.ShapeDtypeStruct(lead + (rb, D), BF),
+            jax.ShapeDtypeStruct(lead + (8, 128), F32),
+            jax.ShapeDtypeStruct((MICRO, count * rows, D), BF),
+            jax.ShapeDtypeStruct((MICRO, count * erows, D), BF),
+            jax.ShapeDtypeStruct((MICRO, HALO, D), BF),
+        ],
+        scratch_shapes=[
+            dma((18,)), dma((units, d)), dma((units, d)),
+            dma((3, 2, count)), dma((3, 2, count)), dma(()), dma(()),
+        ],
+        compiler_params=pltpu.CompilerParams(
+            collective_id=0, has_side_effects=True, vmem_limit_bytes=60 * MIB
+        ),
+        name="gather",
+    )(*shards, small, tok, enc, cot)
+
+
+def reduce_kernel(n, count, rows, erows, *refs):
+    grads = refs[0:3]
+    part, genc, own = refs[3:6]
+    outs = refs[6:9]
+    tok_out, enc_out = refs[9:11]
+    rest = list(refs[11:])
+    d = bit_count(n)
+
+    def take(k):
+        got = rest[:k]
+        del rest[:k]
+        return got
+
+    accs, zls, zrs, zss, fins = take(3), take(3), take(3), take(3), take(3)
+    recvs = [take(d) for _ in range(3)]
+    tbuf, ebuf = take(2)
+    fsend, frecv, zsend, zrecv, tsend, trecv, esend, erecv = rest
+    me, bits = my_place(n)
+    rank = lax.axis_index("seq")
+    last = count - 1
+    peers = [("fsdp", partner_of(me, bits, b), None) for b in range(d)]
+    peers += [("seq", lax.rem(rank + k, count), None) for k in range(1, count)]
+    greet(peers)
+
+    moves = []
+    for k in range(1, count):
+        to = lax.rem(rank + k, count)
+        for m in range(MICRO):
+            moves.append(
+                pltpu.make_async_remote_copy(
+                    src_ref=part.at[m, pl.ds(pl.multiple_of(to * rows, 16), rows)],
+                    dst_ref=tbuf.at[k - 1, m],
+                    send_sem=tsend.at[k - 1, m], recv_sem=trecv.at[k - 1, m],
+                    device_id={"seq": to}, device_id_type=MESH_ID,
+                )
+            )
+        moves.append(
+            pltpu.make_async_remote_copy(
+                src_ref=genc.at[:, pl.ds(pl.multiple_of(to * erows, 16), erows)],
+                dst_ref=ebuf.at[k - 1],
+                send_sem=esend.at[k - 1], recv_sem=erecv.at[k - 1],
+                device_id={"seq": to}, device_id_type=MESH_ID,
+            )
+        )
+
+    units = weight_units(n)
+    units = units[2:] + units[:2] + [(2, 0, 8, 0, 128, 0)]
+    order_list = [o[::-1] for o in orders(n)]
+
+    def hop(u, phase):
+        array, r0, nr, c0, nc, which = units[u]
+        order = order_list[which]
+        b = order[phase]
+        free = [x for x in range(d) if x not in order[: phase + 1]]
+        cut = (pl.ds(r0, nr), pl.ds(c0, nc))
+        index = at_bits(bits, free, {b: 1 - bits[b]})
+        src = grads[array].at[index + cut] if phase == 0 else accs[array].at[index[:-1] + cut]
+        dst = recvs[array][phase].at[(slice(None),) * len(free) + cut]
+        return pltpu.make_async_remote_copy(
+            src_ref=src, dst_ref=dst, send_sem=fsend.at[u, phase], recv_sem=frecv.at[u, phase],
+            device_id={"fsdp": partner_of(me, bits, b)}, device_id_type=MESH_ID,
+        )
+
+    def add(u, phase):
+        array, r0, nr, c0, nc, which = units[u]
+        order = order_list[which]
+        free = [x for x in range(d) if x not in order[: phase + 1]]
+        cut = (slice(r0, r0 + nr), slice(c0, c0 + nc))
+        index = at_bits(bits, free)
+        base = grads[array][index + cut] if phase == 0 else accs[array][index[:-1] + cut]
+        more = recvs[array][phase][(slice(None),) * len(free) + cut]
+        accs[array][index[:-1] + cut] = (base.astype(F32) + more.astype(F32)).astype(base.dtype)
+
+    here = at_bits(bits, ())[:-1]
+
+    def root_of(which):
+        return (count - 1) // 2 if which == 0 else count // 2
+
+    def z_copy(u, kind, src, dst, target):
+        return pltpu.make_async_remote_copy(
+            src_ref=src, dst_ref=dst, send_sem=zsend.at[u, kind], recv_sem=zrecv.at[u, kind],
+            device_id={"seq": target}, device_id_type=MESH_ID,
+        )
+
+    def z_refs(u):
+        array, r0, nr, c0, nc, which = units[u]
+        cut = (pl.ds(r0, nr), pl.ds(c0, nc))
+        return [x[array].at[cut] for x in (zss, zls, zrs, fins)], root_of(which)
+
+    def z_in(u):
+        array, r0, nr, c0, nc, which = units[u]
+        cut = (slice(r0, r0 + nr), slice(c0, c0 + nc))
+        (zs, zl, zr, fin), root = z_refs(u)
+        zss[array][cut] = accs[array][here + cut]
+
+        @pl.when((rank > 0) & (rank <= root))
+        def _():
+            z_copy(u, 0, zs, zl, rank - 1).wait_recv()
+            zss[array][cut] = (
+                zss[array][cut].astype(F32) + zls[array][cut].astype(F32)
+            ).astype(zss[array].dtype)
+
+        @pl.when((rank < last) & (rank >= root))
+        def _():
+            z_copy(u, 1, zs, zr, rank + 1).wait_recv()
+            zss[array][cut] = (
+                zss[array][cut].astype(F32) + zrs[array][cut].astype(F32)
+            ).astype(zss[array].dtype)
+
+        @pl.when(rank < root)
+        def _():
+            z_copy(u, 0, zs, zl, rank + 1).start()
+
+        @pl.when(rank > root)
+        def _():
+            z_copy(u, 1, zs, zr, rank - 1).start()
+
+        @pl.when(rank == root)
+        def _():
+            fins[array][cut] = zss[array][cut]
+
+        @pl.when((rank == root) & (rank > 0))
+        def _():
+            z_copy(u, 2, fin, fin, rank - 1).start()
+
+        @pl.when((rank == root) & (rank < last))
+        def _():
+            z_copy(u, 3, fin, fin, rank + 1).start()
+
+    def z_out(u):
+        array, r0, nr, c0, nc, which = units[u]
+        (zs, zl, zr, fin), root = z_refs(u)
+
+        @pl.when(rank < root)
+        def _():
+            z_copy(u, 2, fin, fin, rank + 1).wait_recv()
+
+        @pl.when((rank < root) & (rank > 0))
+        def _():
+            z_copy(u, 2, fin, fin, rank - 1).start()
+
+        @pl.when(rank > root)
+        def _():
+            z_copy(u, 3, fin, fin, rank - 1).wait_recv()
+
+        @pl.when((rank > root) & (rank < last))
+        def _():
+            z_copy(u, 3, fin, fin, rank + 1).start()
+
+        cut = (slice(r0, r0 + nr), slice(c0, c0 + nc))
+        outs[array][cut] = fins[array][cut].astype(F32)
+
+    def z_sent(u):
+        (zs, zl, zr, fin), root = z_refs(u)
+
+        @pl.when(rank < root)
+        def _():
+            z_copy(u, 0, zs, zl, rank + 1).wait_send()
+
+        @pl.when(rank > root)
+        def _():
+            z_copy(u, 1, zs, zr, rank - 1).wait_send()
+
+        @pl.when((rank <= root) & (rank > 0))
+        def _():
+            z_copy(u, 2, fin, fin, rank - 1).wait_send()
+
+        @pl.when((rank >= root) & (rank < last))
+        def _():
+            z_copy(u, 3, fin, fin, rank + 1).wait_send()
+
+    for u in range(len(units)):
+        hop(u, 0).start()
+    for move in moves:
+        move.start()
+    lag = 4
+    for t in range(len(units) + d + lag + 1):
+        for stage in range(d + 2):
+            u = t - stage - (lag if stage == d + 1 else 0)
+            if not 0 <= u < len(units):
+                continue
+            if stage < d:
+                hop(u, stage).wait_recv()
+                add(u, stage)
+                if stage + 1 < d:
+                    hop(u, stage + 1).start()
+            elif stage == d:
+                z_in(u)
+            else:
+                z_out(u)
+    for move in moves:
+        move.wait_recv()
+    mine = pl.ds(pl.multiple_of(rank * rows, 16), rows)
+    emine = pl.ds(pl.multiple_of(rank * erows, 16), erows)
+    for m in range(MICRO):
+        total = own[m] + part[m, mine, :].astype(F32)
+        states = genc[m, emine, :].astype(F32)
+        for k in range(1, count):
+            total = total + tbuf[k - 1, m].astype(F32)
+            states = states + ebuf[k - 1, m].astype(F32)
+        tok_out[m] = total
+        enc_out[m] = states
+    for move in moves:
+        move.wait_send()
+    for u in range(len(units)):
+        for phase in range(d):
+            hop(u, phase).wait_send()
+        z_sent(u)
+
+
+def reduce_out(n, count, ga, gb, gs, part, genc, own):
+    rows = own.shape[1]
+    erows = genc.shape[1] // count
+    d = bit_count(n)
+    units = len(weight_units(n)) + 1
+    dma = pltpu.SemaphoreType.DMA
+    V = pltpu.VMEM
+    grads = (ga, gb, gs)
+    flat = [(g.shape[-2], g.shape[-1]) for g in grads]
+    types = [g.dtype for g in grads]
+    scratch = [V((2,) * (d - 1) + f, t) for f, t in zip(flat, types)]
+    for _ in range(4):
+        scratch += [V(f, t) for f, t in zip(flat, types)]
+    for f, t in zip(flat, types):
+        scratch += [V((2,) * (d - 1 - p) + f, t) for p in range(d)]
+    scratch += [V((count - 1, MICRO, rows, D), BF), V((count - 1, MICRO, erows, D), BF)]
+    scratch += [
+        dma((units, d)), dma((units, d)), dma((units, 4)), dma((units, 4)),
+        dma((count - 1, MICRO)), dma((count - 1, MICRO)), dma((count - 1,)), dma((count - 1,)),
+    ]
+    return pl.pallas_call(
+        functools.partial(reduce_kernel, n, count, rows, erows),
+        in_specs=[VM] * 6,
+        out_specs=[VM] * 5,
+        out_shape=[jax.ShapeDtypeStruct(f, F32) for f in flat]
+        + [jax.ShapeDtypeStruct((MICRO, rows, D), F32), jax.ShapeDtypeStruct((MICRO, erows, D), F32)],
+        scratch_shapes=scratch,
+        compiler_params=pltpu.CompilerParams(
+            collective_id=1, has_side_effects=True, vmem_limit_bytes=60 * MIB
+        ),
+        name="reduce_out",
+    )(ga, gb, gs, part, genc, own)
 
 
 def on_device(
@@ -515,6 +1055,7 @@
     gain_one, shift_one, gain_two, shift_two, gain_three, shift_three, w_slot,
 ):
     n = lax.axis_size("fsdp")
+    count = lax.axis_size("seq")
     rank = lax.axis_index("seq")
     tokens = tokens[:, 0]
     rows = tokens.shape[1]
@@ -525,21 +1066,21 @@
     cot = cotangent[:, 0]
 
     shards = (w_query, w_key, w_value, w_out, c_query, c_key, c_value, c_out, w_up, w_down, w_slot)
-    full = [lax.all_gather(w, "fsdp", axis=0, tiled=False) for w in shards]
-    wq, wk, wv, wout, cq, ck, cv, cout, up, down, slot = full
+    edge, side = FF // n, D // n
     small = jnp.concatenate(
         [b_up, b_down, gain_one, shift_one, gain_two, shift_two, gain_three, shift_three]
+    ).astype(F32)
+    small = jnp.pad(small, (0, 1024 - small.shape[0])).reshape(8, 128)
+    wa, wb, small_all, x_all, e_all, previous = gather(
+        n, count, shards, small, tokens, encoded[:, 0], cot
     )
-    small_all = lax.all_gather(small, "fsdp", axis=0, tiled=False)
-    edge = FF // n
-    bup = small_all[:, :edge].reshape(1, FF).astype(F32)
-    vecs = small_all[:, edge:].reshape(n, 7, D // n).transpose(1, 0, 2).reshape(7, D).astype(F32)
+    wa = wa.reshape((n,) + wa.shape[-2:])
+    wb = wb.reshape((n,) + wb.shape[-2:])
+    small_all = small_all.reshape(n, 1024)
+    bup = small_all[:, :edge].reshape(1, FF)
+    vecs = small_all[:, edge : edge + 7 * side].reshape(n, 7, side).transpose(1, 0, 2).reshape(7, D)
     vecs = jnp.concatenate([vecs, jnp.zeros((1, D), F32)], axis=0)
-
-    x_all = lax.all_gather(tokens, "seq", axis=1, tiled=True)
-    e_all = lax.all_gather(encoded[:, 0], "seq", axis=1, tiled=True)
-    previous = passed_along(cot[:, rows - HALO :], "seq", 1)[:, HALO - 1 :]
-    shifted = jnp.concatenate([previous, cot[:, : rows - 1]], axis=1)
+    shifted = jnp.concatenate([previous[:, HALO - 1 :], cot[:, : rows - 1]], axis=1)
 
     numbers = jnp.arange(1, prefix.shape[1] + 1, dtype=jnp.int32)
     limit = jnp.sum(
@@ -563,41 +1104,39 @@
     start = jnp.minimum(offset + rows, glen - HALO)
     x_ext = jnp.concatenate([tokens, lax.dynamic_slice_in_dim(x_all, start, HALO, 1)], axis=1)
 
-    q, k, v, mix, lse = self_forward(x_all, wq, wk, wv, col, row[:, 1:2], rows)
-    (
-        slot_out, dmix, dr1, genc,
-        g_out, g_cq, g_ck, g_cv, g_cout, g_up, g_down, g_slot, g_bup, g_vec,
-    ) = middle(mix, x_ext, e_all, cot, shifted, flags, (wout, cq, ck, cv, cout, up, down, slot), bup, vecs, rows)
-    own, part, g_q, g_k, g_v = self_backward(
-        x_all, q, k, v, mix, dmix, dr1, lse, row, wq, wk, wv, rows
+    q, k, v, mix, lse = self_forward(x_all, wa, col, row[:, 1:2], rows)
+    slot_out, dmix, dr1, genc, gb, g_bup, g_vec = middle(
+        mix, x_ext, e_all, cot, shifted, flags, wb, bup, vecs, rows
     )
-
-    grad_tokens = own + lax.psum_scatter(part, "seq", scatter_dimension=1, tiled=True).astype(F32)
-    grad_encoded = lax.psum_scatter(genc, "seq", scatter_dimension=1, tiled=True).astype(F32)
-    grads = (g_q, g_k, g_v, g_out, g_cq, g_ck, g_cv, g_cout, g_up, g_down, g_slot)
-
-    def reduced(g):
-        g = lax.psum_scatter(g, "fsdp", scatter_dimension=0, tiled=False)
-        return lax.psum(g, "seq").astype(F32)
-
-    (g_q, g_k, g_v, g_out, g_cq, g_ck, g_cv, g_cout, g_up, g_down, g_slot) = [reduced(g) for g in grads]
-    packed = jnp.concatenate(
+    own, part, ga = self_backward(x_all, q, k, v, mix, dmix, dr1, lse, row, wa, rows)
+
+    gs = jnp.concatenate(
         [
-            g_bup[0:1].reshape(n, FF // n),
-            g_vec[:7].reshape(7, n, D // n).transpose(1, 0, 2).reshape(n, 7 * (D // n)),
+            g_bup[0:1].reshape(n, edge),
+            g_vec[:7].reshape(7, n, side).transpose(1, 0, 2).reshape(n, 7 * side),
+            jnp.zeros((n, 1024 - edge - 7 * side), F32),
         ],
         axis=1,
     )
-    packed = lax.psum(packed, ("fsdp", "seq"))
-    mine = lax.dynamic_slice_in_dim(packed, lax.axis_index("fsdp"), 1, 0)[0]
-    b_up_g = mine[:edge]
+    lead = (2,) * bit_count(n)
+    ga = ga.reshape(lead + ga.shape[1:])
+    gb = gb.reshape(lead + gb.shape[1:])
+    gs = gs.reshape(lead + (8, 128))
+    oa, ob, os, grad_tokens, grad_encoded = reduce_out(n, count, ga, gb, gs, part, genc, own)
+    table_a, _ = qkv_rows(n)
+    table_b, _ = rest_rows(n)
+    g = {name: oa[start : start + size] for name, (start, size) in table_a.items()}
+    g.update({name: ob[start : start + size] for name, (start, size) in table_b.items()})
+    g["up"] = g["up"].reshape(4, side, D).transpose(1, 0, 2).reshape(side, FF)
+    line = os.reshape(1024)
+    b_up_g = line[:edge]
     b_down_g, g1, s1, g2, s2, g3, s3 = [
-        mine[edge + i * (D // n) : edge + (i + 1) * (D // n)] for i in range(7)
+        line[edge + i * side : edge + (i + 1) * side] for i in range(7)
     ]
     return (
         slot_out[:, None], grad_tokens[:, None], grad_encoded[:, None],
-        g_q, g_k, g_v, g_out, g_cq, g_ck, g_cv, g_cout,
-        g_up, b_up_g, g_down, b_down_g, g1, s1, g2, s2, g3, s3, g_slot,
+        g["wq"], g["wk"], g["wv"], g["wout"], g["cq"], g["ck"], g["cv"], g["cout"],
+        g["up"], b_up_g, g["down"], b_down_g, g1, s1, g2, s2, g3, s3, g["slot"],
     )
 
 

time: 903 us -> 477 us (0.53)
  waiting for transfers between devices: 518 us -> 0 us
  Pallas kernels: 143 us -> 453 us
  blocking collectives: 172 us -> 0 us
  other arithmetic: 22.5 us -> 6.69 us
  between operations: 15.2 us -> 0.97 us
    reduce_scatter x13 -> x0, waiting for transfers between devices: 467 us -> none  [the longest x11 416 us: reduced(): g = lax.psum_scatter(g, 'fsdp', scatter_dimension=0, tiled=False)]
    pallas_call x0 -> x2, Pallas kernels: none -> 309 us  [the longest x1 189 us: reduce_out(): pl.pallas_call(functools.partial(reduce_kernel, n, count, rows, erows), i...]
    all_gather x9 -> x0, blocking collectives: 107 us -> none  [the longest x8 89.3 us: on_device(): full = [lax.all_gather(w, 'fsdp', axis=0, tiled=False) for w in shards]]
    psum x1 -> x0, waiting for transfers between devices: 41.8 us -> none  [reduced(): return lax.psum(g, 'seq').astype(F32)]
    psum x1 -> x0, blocking collectives: 39.9 us -> none  [on_device(): packed = lax.psum(packed, ('fsdp', 'seq'))]
    unnamed x1 -> x0, blocking collectives: 25.4 us -> none
    convert_element_type x11 -> x0, other arithmetic: 9.83 us -> none  [reduced(): return lax.psum(g, 'seq').astype(F32)]
    unnamed x18 -> x0, waiting for transfers between devices: 9.22 us -> none
  transfers between devices with their start and end apart: 19 -> 0, of which waited for: 13 -> 0; matrix products, arithmetic and copies ran while one was open for 5% -> 0% of each run, Pallas kernels for 4% -> 0%
where the time goes in v2:
time: 477 us
  Pallas kernels  453 us (95%)
  local copies, waits for them, and re-layouts  15.7 us (3%)
  other arithmetic  6.69 us (1%)
    pallas_call x1, Pallas kernels, reduce_out(): pl.pallas_call(functools.partial(reduce_kernel, n, count, rows, erows), i...  189 us
    pallas_call x1, Pallas kernels, gather(): pl.pallas_call(functools.partial(gather_kernel, n, count, rows, erows), i...  119 us
    pallas_call x1, Pallas kernels, self_backward(): pl.pallas_call(functools.partial(self_backward_kernel, glen, rows), in_sp...  64.7 us
    pallas_call x1, Pallas kernels, middle(): pl.pallas_call(functools.partial(middle_kernel, rows, enc), in_specs=[VM]...  47.1 us
    pallas_call x1, Pallas kernels, self_forward(): pl.pallas_call(functools.partial(self_forward_kernel, glen, rows), grid=(...  33.1 us

profile of v2, /device:TPU:0, one launch (start us, length us, event | category | flops | bytes accessed | tf_op | source)
XLA Modules:
  0.0 476.8 jit_solution(16600056691959838179)
XLA Ops:
  0.7 0.8 copy.122
  2.2 0.9 pad_maximum_fusion.2.flag_ref
  3.9 119.0 %gather.1 = (bf16[2,2,2,192,512]{4,3,2,1,0:T(8,128)(2,1)}, bf16[2,2,2,960,512]{4,3,2,1,0:T(8,128)(2,1)}, f32[2,2,2,8,128]{4,3,2,1,0:T(8,128)}, bf16[2,1536,512]{...) custom-call(bf16[64,512]{1,0:T(8,128)(2,1)} %refs_0_.1, bf16[64,512]{1,0:T(8,128)(2,1)} %refs_1_.1, ...), custom_call_target="tpu_custom_call" | custom-call | tf_op jit(solution)/shard_map/gather/pallas_call | solution.py:784
  124.7 1.6 pad_add_fusion.col_ref
  126.3 33.1 %self_forward.1 = (bf16[2,400,512]{2,1,0:T(8,128)(2,1)}, bf16[2,1536,512]{2,1,0:T(8,128)(2,1)}, bf16[2,1536,512]{2,1,0:T(8,128)(2,1)}, bf16[2,400,512]{2,1,0:T(8,128)(2,1)}, f32[2,8,384]{2,1,0:T(8,128)}) custom-call(bf16[2,1536,512]{2,1,0:T(8,128)(2,1)} %get-tuple-element.48.x_ref, bf16[8,192,512]{2,1,0:T(8,128)(2,1)} %bitcast.60, ...), custom_call_target="tpu_custom_call" | custom-call | tf_op jit(solution)/shard_map/self_forward/pallas_call | solution.py:200
  159.4 0.9 constant_dynamic-slice_fusion
  160.3 1.0 pad_maximum_fusion.x_ref
  161.3 0.7 slice.84
  162.0 1.1 pad_maximum_fusion.1.shifted_ref
  163.3 0.6 concatenate.22.vec_ref
  163.9 0.6 copy.115
  164.5 47.1 %middle.1 = (bf16[2,384,512]{2,1,0:T(8,128)(2,1)}, bf16[2,384,512]{2,1,0:T(8,128)(2,1)}, f32[2,384,512]{2,1,0:T(8,128)}, bf16[2,256,512]{2,1,0:T(8,128)(2,1)}, b...) custom-call(bf16[2,400,512]{2,1,0:T(8,128)(2,1)} %get-tuple-element.50.mix_ref, ...), custom_call_target="tpu_custom_call" | custom-call | tf_op jit(solution)/shard_map/middle/pallas_call | solution.py:446
  211.7 0.8 reshape.129
  212.5 0.9 slice_reduce_fusion
  213.5 0.6 copy.116
  214.1 0.6 pad_add_fusion.1.row_ref
  214.8 64.7 %self_backward.1 = (f32[2,384,512]{2,1,0:T(8,128)}, bf16[2,1536,512]{2,1,0:T(8,128)(2,1)}, bf16[8,192,512]{2,1,0:T(8,128)(2,1)}) custom-call(bf16[2,1536,512]{2,1,0:T(8,128)(2,1)} %get-tuple-element.48.x_ref, bf16[2,400,512]{2,1,0:T(8,128)(2,1)} %get-tuple-element.56.q_ref, bf16[2,1536,512]{2,1,0:T(8,128)(2,1)} %get-tuple-element.57.k_ref, ...), custom_call_target="tpu_custom_call" | custom-call | tf_op jit(solution)/shard_map/self_backward/pallas_call | solution.py:546
  279.5 189.5 %reduce_out.1 = (f32[192,512]{1,0:T(8,128)}, f32[960,512]{1,0:T(8,128)}, f32[8,128]{1,0:T(8,128)}, f32[2,384,512]{2,1,0:T(8,128)}, f32[2,64,512]{2,1,0:T(8,128)}) custom-call(bf16[2,2,2,192,512]{4,3,2,1,0:T(8,128)(2,1)} %bitcast.65, bf16[2,2,2,960,512]{4,3,2,1,0:T(8,128)(2,1)} %bitcast.56, f32[2,2,2,8,128]{4,3,2,1,0:T(8,128)} %bitcast.71, ...), custom_call_target="tpu_custom_call" | custom-call | tf_op jit(solution)/shard_map/reduce_out/pallas_call | solution.py:1037
  469.0 2.4 fusion.1
  471.4 0.9 fusion
  472.3 0.8 copy.113
  473.1 0.7 slice.111
  475.0 1.1 copy.125
  476.1 0.7 copy.126
  (64 shorter events, 4.6 us)
Async XLA Ops:
  0.7 2.5 copy-start.10
  0.7 2.4 copy-start.11
  0.7 2.4 copy-start.12
  0.7 2.4 copy-start.13
  0.7 2.4 copy-start.14
  0.7 2.4 copy-start.15
  0.7 2.4 copy-start.16
  0.7 2.4 copy-start.17
  3.1 119.8 %copy-start.9 = (s32[2,1,4]{2,1,0:T(1,128)S(1)}, s32[2,1,4]{2,1,0:T(1,128)}, u32[]{:S(2)}) copy-start(s32[2,1,4]{2,1,0:T(1,128)} %param.27) | copy-start | bytes 100
  3.1 119.9 %copy-start.5 = (s32[2,1,1536]{2,1,0:T(1,128)S(1)}, s32[2,1,1536]{2,1,0:T(1,128)}, u32[]{:S(2)}) copy-start(s32[2,1,1536]{2,1,0:T(1,128)} %row_ref.1) | copy-start | bytes 36868
  126.3 34.0 %copy-start.1 = (bf16[2,1,384,512]{3,2,1,0:T(8,128)(2,1)S(1)}, bf16[2,1,384,512]{3,2,1,0:T(8,128)(2,1)}, u32[]{:S(2)}) copy-start(bf16[2,1,384,512]{3,2,1,0:T(8,128)(2,1)} %param.24) | copy-start | bytes 2359300
  159.4 2.6 copy-start
  160.3 2.8 copy-start.7
  164.5 49.6 %copy-start.6 = (s32[2,1,1536]{2,1,0:T(1,128)S(1)}, s32[2,1,1536]{2,1,0:T(1,128)}, u32[]{:S(2)}) copy-start(s32[2,1,1536]{2,1,0:T(1,128)} %row_ref.1) | copy-start | bytes 36868
  469.0 2.4 copy-start.2
  471.4 2.4 copy-start.8
  471.4 3.6 copy-start.3
  475.0 1.1 copy-start.4

commit v3 on v2

--- a/solution.py
+++ b/solution.py
@@ -146,73 +146,24 @@
 
 MESH_ID = pl.DeviceIdType.MESH
 
-
-def self_forward_kernel(
-    glen, rows, x_ref, w_ref, col_ref, row_ref,
-    q_ref, k_ref, v_ref, mix_ref, lse_out, bias, lse_sc,
-):
+def place_info(info, seg_ref, prefix_ref, m):
+    glen = info.shape[1]
     prompt = glen // 3
-    rank = lax.axis_index("seq")
-    off = pl.multiple_of(rank * rows, 128)
-    edge = pl.multiple_of(jnp.minimum(rank * rows + rows, glen - HALO), HALO)
-    table, _ = qkv_rows(w_ref.shape[0])
-    wq, wk, wv = [square(w_ref, table, name) for name in ("wq", "wk", "wv")]
-
-    def project(tile, _):
-        at = pl.ds(pl.multiple_of(tile * 256, 256), 256)
-        part = x_ref[0, at, :]
-        k_ref[0, at, :] = nn(part, wk).astype(BF)
-        v_ref[0, at, :] = nn(part, wv).astype(BF)
-        return 0
-
-    lax.fori_loop(0, glen // 256, project, 0)
-    q_ref[0, 0:rows, :] = (nn(x_ref[0, pl.ds(off, rows), :], wq).astype(BF) * SCALE).astype(BF)
-    q_ref[0, rows : rows + HALO, :] = (
-        nn(x_ref[0, pl.ds(edge, HALO), :], wq).astype(BF) * SCALE
-    ).astype(BF)
-    seg_row = row_ref[0, 0:1, :]
-    place = lax.broadcasted_iota(jnp.int32, (1, glen), 1)
-    for start, count, src in ((0, rows, off), (rows, HALO, edge)):
-        info = col_ref[0, pl.ds(src, count), :]
-        limit = info[:, 0:1]
-        seg = info[:, 1:2]
-        seen = jnp.where(place < prompt, (place < limit).astype(jnp.int32), (seg_row == seg).astype(jnp.int32))
-        bias[start : start + count, :] = jnp.where(seen == 1, 0.0, NEG)
-
-    def one_pair(pair, _):
-        at = lanes_of(pair)
-        mix = attend_pair(q_ref[0, :, at], k_ref[0, :, at], v_ref[0, :, at], bias[...], pair, lse_sc)
-        mix_ref[0, :, at] = mix.astype(BF)
-        return 0
-
-    lax.fori_loop(0, HEADS // 2, one_pair, 0)
-    lse_out[0] = lse_sc[0:rows, :].T[0:HEADS, :]
-
-
-def self_forward(x_all, w, col, row, rows):
-    glen = x_all.shape[1]
-    ext = rows + HALO
-    weight = pl.BlockSpec(w.shape, lambda m: (0, 0, 0))
-
-    def micro(*shape):
-        return pl.BlockSpec((1,) + shape, lambda m: (m, 0, 0))
-
-    return pl.pallas_call(
-        functools.partial(self_forward_kernel, glen, rows),
-        grid=(MICRO,),
-        in_specs=[micro(glen, D), weight, micro(glen, 2), micro(1, glen)],
-        out_specs=[micro(ext, D), micro(glen, D), micro(glen, D), micro(ext, D), micro(HEADS, rows)],
-        out_shape=[
-            jax.ShapeDtypeStruct((MICRO, ext, D), BF),
-            jax.ShapeDtypeStruct((MICRO, glen, D), BF),
-            jax.ShapeDtypeStruct((MICRO, glen, D), BF),
-            jax.ShapeDtypeStruct((MICRO, ext, D), BF),
-            jax.ShapeDtypeStruct((MICRO, HEADS, rows), F32),
-        ],
-        scratch_shapes=[pltpu.VMEM((ext, glen), F32), pltpu.VMEM((ext, 128), F32)],
-        compiler_params=pltpu.CompilerParams(vmem_limit_bytes=56 * MIB),
-        name="self_forward",
-    )(x_all, w, col, row)
+    seg = jnp.broadcast_to(seg_ref[m], (8, glen))
+    limit = jnp.where(seg == 0, prompt, 0)
+    for c in range(prefix_ref.shape[1]):
+        limit = jnp.where(seg == c + 1, prefix_ref[m, c], limit)
+    place = lax.broadcasted_iota(jnp.int32, (8, glen), 1)
+    after = (seg == pltpu.roll(seg, glen - 1, 1)) & (place < glen - 1)
+    before = (seg == pltpu.roll(seg, 1, 1)) & (place > 0)
+    sub = lax.broadcasted_iota(jnp.int32, (8, glen), 0)
+    mixed = jnp.where(sub == 0, limit, seg)
+    mixed = jnp.where(sub == 2, after.astype(jnp.int32), mixed)
+    mixed = jnp.where(sub == 3, before.astype(jnp.int32), mixed)
+    info[...] = mixed.astype(F32)
+
+
+SMEM = pl.BlockSpec(memory_space=pltpu.SMEM)
 
 
 def norm_forward(residual, gain, shift):
@@ -254,11 +205,11 @@
 
 def middle_kernel(
     rows, enc,
-    mix_ref, x_ref, e_ref, cot_ref, shifted_ref, flag_ref,
+    mix_ref, x_ref, edge_ref, e_ref, cot_ref, prev_ref, seg_ref, prefix_ref,
     w_ref, bup_ref, vec_ref,
     slot_out, dmix_out, dr1_out, genc_out, g_ref, gbup, gvec,
     lowx, lown, cqs, cks, cvs, lse_sc, lse_row, cmix, h1s, hats, rstds, slope,
-    act, dpre, dffn, dcross, dcqs, dattn, dcks, dcvs, ckt, h3s, h2low,
+    act, dpre, dffn, dcross, dcqs, dattn, dcks, dcvs, ckt, h3s, h2low, info, shs,
 ):
     ext = rows + HALO
     table, _ = rest_rows(w_ref.shape[0])
@@ -271,7 +222,8 @@
     def one_micro(m, _):
         own = pl.ds(0, rows)
         attn = nn(mix_ref[m], square(w_ref, table, "wout"))
-        h1, hat, rstd = norm_forward(x_ref[m].astype(F32) + attn, vec(1), vec(2))
+        x_rows = jnp.concatenate([x_ref[m], edge_ref[m]], axis=0).astype(F32)
+        h1, hat, rstd = norm_forward(x_rows + attn, vec(1), vec(2))
         h1s[...] = h1
         dr1_out[m] = hat[0:rows]
         rstds[:, 0:1] = rstd[0:rows]
@@ -315,10 +267,15 @@
         lown[2, m] = h3_low[0:rows]
         top = row_part(w_ref, table, "slot", 0)
         bottom = row_part(w_ref, table, "slot", 1)
-        flags = flag_ref[m]
-        follow = (h3s[pl.ds(1, rows), :] * flags[:, 0:1]).astype(BF)
+        place_info(info, seg_ref, prefix_ref, m)
+        flags = info[:, pl.ds(pl.multiple_of(lax.axis_index("seq") * rows, 128), rows)].T
+        follow = (h3s[pl.ds(1, rows), :] * flags[:, 2:3]).astype(BF)
         slot_out[m] = (nn(h3_low[0:rows], top) + nn(follow, bottom)).astype(BF)
-        d_follow = nt(shifted_ref[m], bottom).astype(BF).astype(F32) * flags[:, 1:2]
+        h3s[0:8, :] = prev_ref[m].astype(F32)[HALO - 8 : HALO]
+        h3s[8 : rows + 8, :] = cot_ref[m].astype(F32)
+        shifted = h3s[pl.ds(7, rows), :]
+        shs[m] = (shifted * flags[:, 3:4]).astype(BF)
+        d_follow = nt(shifted.astype(BF), bottom).astype(BF).astype(F32) * flags[:, 3:4]
         d_three = nt(cot_ref[m], top) + d_follow
         d_r3, d_gain, d_shift = norm_backward(d_three, hat[0:rows], rstd[0:rows], vec(5))
         gvec[5:6, :] += d_gain
@@ -393,9 +350,7 @@
         return tn(left, right).astype(BF)
 
     cot = cot_ref[...].reshape(total, D)
-    flagged = jnp.concatenate(
-        [(shifted_ref[m].astype(F32) * flag_ref[m][:, 1:2]).astype(BF) for m in range(MICRO)], axis=0
-    )
+    flagged = shs[...].reshape(total, D)
     h3_all = lown[2].reshape(total, D)
     store_part(g_ref, table, "slot", 0, grad_of(h3_all, cot))
     store_part(g_ref, table, "slot", 1, grad_of(h3_all, flagged))
@@ -414,7 +369,8 @@
     store_square(g_ref, table, "wout", grad_of(mix_all, dattn[...].reshape(total, D)))
 
 
-def middle(mix, x_ext, e_all, cot, shifted, flags, w, bup, vecs, rows):
+def middle(mix, tokens, edges, e_all, cot, prev, seg, prefix, w, bup, vecs, rows):
+    glen = seg.shape[2]
     enc = e_all.shape[1]
     ext = rows + HALO
     out_shape = [
@@ -442,23 +398,24 @@
         V((MICRO, enc, D), BF), V((MICRO, enc, D), BF),
         V((D, enc), BF),
         V((ext, D), F32), V((ext, D), BF),
+        V((8, glen), F32), V((MICRO, rows, D), BF),
     ]
     return pl.pallas_call(
         functools.partial(middle_kernel, rows, enc),
-        in_specs=[VM] * 9,
+        in_specs=[VM] * 7 + [SMEM] + [VM] * 3,
         out_specs=[VM] * len(out_shape),
         out_shape=out_shape,
         scratch_shapes=scratch,
         compiler_params=pltpu.CompilerParams(vmem_limit_bytes=60 * MIB),
         name="middle",
-    )(mix, x_ext, e_all, cot, shifted, flags, w, bup, vecs)
+    )(mix, tokens, edges, e_all, cot, prev, seg, prefix, w, bup, vecs)
 
 
 def self_backward_kernel(
     glen, rows,
-    x_ref, q_ref, k_ref, v_ref, mix_ref, dmix_ref, dr1_ref, lse_ref, row_ref,
+    x_ref, q_ref, k_ref, v_ref, mix_ref, dmix_ref, dr1_ref, lse_ref, seg_ref, prefix_ref,
     w_ref, own_out, part_out, g_ref,
-    bias, stats, dqt, dqs, dks, dvs,
+    bias, stats, dqt, dqs, dks, dvs, info,
 ):
     prompt = glen // 3
     tile = 256
@@ -467,15 +424,16 @@
     off = pl.multiple_of(rank * rows, 128)
 
     def one_micro(m, _):
-        limit = row_ref[m, 0:1, pl.ds(off, rows)]
-        seg = row_ref[m, 1:2, pl.ds(off, rows)]
+        place_info(info, seg_ref, prefix_ref, m)
+        limit = info[0:1, pl.ds(off, rows)]
+        seg = info[1:2, pl.ds(off, rows)]
 
         def masks(t, _):
             at = pl.ds(pl.multiple_of(t * tile, tile), tile)
             place = lax.broadcasted_iota(jnp.int32, (tile, 1), 0) + t * tile
-            key_seg = jnp.broadcast_to(row_ref[m, 1:2, at], (8, tile)).T[:, 0:1]
+            key_seg = info[:, at].T[:, 1:2]
             seen = jnp.where(
-                place < prompt, (place < limit).astype(jnp.int32), (key_seg == seg).astype(jnp.int32)
+                place < prompt, (place.astype(F32) < limit).astype(jnp.int32), (key_seg == seg).astype(jnp.int32)
             )
             bias[at, :] = jnp.where(seen == 1, 0.0, NEG)
             return 0
@@ -540,12 +498,12 @@
     store_square(g_ref, table, "wv", tn(x_all, dvs[...].reshape(MICRO * glen, D)).astype(BF))
 
 
-def self_backward(x_all, q, k, v, mix, dmix, dr1, lse, row, w, rows):
+def self_backward(x_all, q, k, v, mix, dmix, dr1, lse, seg, prefix, w, rows):
     glen = x_all.shape[1]
     V = pltpu.VMEM
     return pl.pallas_call(
         functools.partial(self_backward_kernel, glen, rows),
-        in_specs=[VM] * 10,
+        in_specs=[VM] * 9 + [SMEM, VM],
         out_specs=[VM] * 3,
         out_shape=[
             jax.ShapeDtypeStruct((MICRO, rows, D), F32),
@@ -555,59 +513,11 @@
         scratch_shapes=[
             V((glen, rows), F32), V((2 * HEADS, rows), F32), V((128, rows), F32),
             V((MICRO, rows, D), BF), V((MICRO, glen, D), BF), V((MICRO, glen, D), BF),
+            V((8, glen), F32),
         ],
         compiler_params=pltpu.CompilerParams(vmem_limit_bytes=60 * MIB),
         name="self_backward",
-    )(x_all, q, k, v, mix, dmix, dr1, lse, row, w)
-
-
-class Chain:
-    def __init__(self, ref, rows, sems, lane, rank, count):
-        self.ref, self.rows, self.lane = ref, rows, lane
-        self.send, self.recv = sems
-        self.rank, self.count = rank, count
-
-    def copy(self, side, step, block, target):
-        at = pl.ds(pl.multiple_of(block * self.rows, 16), self.rows)
-        part = self.ref.at[:, at] if len(self.ref.shape) == 3 else self.ref.at[at]
-        return pltpu.make_async_remote_copy(
-            src_ref=part, dst_ref=part,
-            send_sem=self.send.at[self.lane, side, step], recv_sem=self.recv.at[self.lane, side, step],
-            device_id={"seq": target}, device_id_type=MESH_ID,
-        )
-
-    def start(self, step):
-        r, last = self.rank, self.count - 1
-
-        @pl.when((r < last) & (r - step >= 0))
-        def _():
-            self.copy(0, step, r - step, r + 1).start()
-
-        @pl.when((r > 0) & (r + step <= last))
-        def _():
-            self.copy(1, step, r + step, r - 1).start()
-
-    def arrived(self, step):
-        r, last = self.rank, self.count - 1
-
-        @pl.when(r - 1 - step >= 0)
-        def _():
-            self.copy(0, step, r - 1 - step, r - 1).wait_recv()
-
-        @pl.when(r + 1 + step <= last)
-        def _():
-            self.copy(1, step, r + 1 + step, r + 1).wait_recv()
-
-    def sent(self, step):
-        r, last = self.rank, self.count - 1
-
-        @pl.when((r < last) & (r - step >= 0))
-        def _():
-            self.copy(0, step, r - step, r + 1).wait_send()
-
-        @pl.when((r > 0) & (r + step <= last))
-        def _():
-            self.copy(1, step, r + step, r - 1).wait_send()
+    )(x_all, q, k, v, mix, dmix, dr1, lse, seg, prefix, w)
 
 
 def weight_units(n):
@@ -641,14 +551,87 @@
     pl.semaphore_wait(barrier, amount if always < len(peers) else always)
 
 
-def gather_kernel(n, count, rows, erows, *refs):
+STRIP = 128
+
+
+def key_span(rank, rows, glen):
+    prompt = glen // 3
+    least = (glen - prompt) // 8
+    most = (glen - prompt) - 3 * least
+    first, stop = rank * rows, (rank + 1) * rows + 1
+    low = jnp.maximum(first - most, jnp.where(first >= prompt + most, prompt + least, prompt))
+    high = jnp.minimum(stop + most, jnp.where(stop <= glen - most, glen - least, glen))
+    return low, jnp.where(stop > prompt, high, 0)
+
+
+class Chain:
+    def __init__(self, ref, rows, strips, sems, lane, rank, count, needed):
+        self.ref, self.rows, self.lane, self.needed = ref, rows, lane, needed
+        self.strips, self.height = strips, rows // strips
+        self.send, self.recv = sems
+        self.rank, self.count = rank, count
+
+    def copy(self, side, step, j, block, target):
+        at = pl.ds(pl.multiple_of(block * self.rows + j * self.height, 16), self.height)
+        part = self.ref.at[:, at] if len(self.ref.shape) == 3 else self.ref.at[at]
+        return pltpu.make_async_remote_copy(
+            src_ref=part, dst_ref=part,
+            send_sem=self.send.at[self.lane, side, step, j],
+            recv_sem=self.recv.at[self.lane, side, step, j],
+            device_id={"seq": target}, device_id_type=MESH_ID,
+        )
+
+    def goes(self, side, sender, block, j):
+        last = self.count - 1
+        if side == 0:
+            there = (sender >= 0) & (sender < last) & (block >= 0)
+            taker = sender + 1
+        else:
+            there = (sender <= last) & (sender > 0) & (block <= last)
+            taker = sender - 1
+        if self.needed is None:
+            return there
+        return there & self.needed(side, taker, block * self.rows + j * self.height, self.height)
+
+    def outgoing(self, step, j, act):
+        r = self.rank
+        for side, block, target in ((0, r - step, r + 1), (1, r + step, r - 1)):
+
+            @pl.when(self.goes(side, r, block, j))
+            def _():
+                act(self.copy(side, step, j, block, target))
+
+    def start(self, step):
+        for j in range(self.strips):
+            self.outgoing(step, j, lambda c: c.start())
+
+    def arrived(self, step, onward):
+        r = self.rank
+        for j in range(self.strips):
+            for side, block, source in ((0, r - 1 - step, r - 1), (1, r + 1 + step, r + 1)):
+
+                @pl.when(self.goes(side, source, block, j))
+                def _():
+                    self.copy(side, step, j, block, source).wait_recv()
+
+            if onward:
+                self.outgoing(step + 1, j, lambda c: c.start())
+
+    def sent(self, step):
+        for j in range(self.strips):
+            self.outgoing(step, j, lambda c: c.wait_send())
+
+
+def front_kernel(n, count, rows, erows, *refs):
     shards = refs[0:11]
-    small, tok, enc, cot = refs[11:15]
-    wa, wb, small_all, x_all, e_all, prev = refs[15:21]
-    local, fsend, frecv, zsend, zrecv, csend, crecv = refs[21:]
+    small, tok, enc, cot, seg_ref, prefix_ref = refs[11:17]
+    wa, wb, small_all, x_all, e_all, prev, halo_out, q_ref, k_ref, v_ref, mix_ref, lse_out = refs[17:29]
+    stage, bias, lse_sc, info, local, fsend, frecv, zsend, zrecv, csend, crecv = refs[29:]
     me, bits = my_place(n)
     rank = lax.axis_index("seq")
     last = count - 1
+    glen = count * rows
+    prompt = glen // 3
     piece = D // n
     d = bit_count(n)
 
@@ -666,16 +649,13 @@
     keep(enc, e_all.at[:, pl.ds(pl.multiple_of(rank * erows, 16), erows)])
     names = ("wq", "wk", "wv", "wout", "cq", "ck", "cv", "cout", "up", "down", "slot")
     for name, shard in zip(names, shards):
-        table, target = (table_a, wa) if name in table_a else (table_b, wb)
-        start, size = table[name]
+        start, size = (table_a if name in table_a else table_b)[name]
+        target = wa.at[here] if name in table_a else stage
         if name == "up":
             for c in range(4):
-                keep(
-                    shard.at[:, pl.ds(c * D, D)],
-                    target.at[here + (pl.ds(start + c * piece, piece), slice(None))],
-                )
+                keep(shard.at[:, pl.ds(c * D, D)], target.at[pl.ds(start + c * piece, piece)])
         else:
-            keep(shard, target.at[here + (pl.ds(start, size), slice(None))])
+            keep(shard, target.at[pl.ds(start, size)])
     keep(small, small_all.at[here])
 
     peers = [("fsdp", partner_of(me, bits, b), None) for b in range(d)]
@@ -686,37 +666,41 @@
     units = weight_units(n) + [(2, 0, 8, 0, 128, 0)]
     order_list = orders(n)
 
-    def hop(u, phase):
+    def hop(u, phase, theirs=False):
         array, r0, nr, c0, nc, which = units[u]
         order = order_list[which]
         b = order[phase]
-        part = arrays[array].at[at_bits(bits, order[:phase]) + (pl.ds(r0, nr), pl.ds(c0, nc))]
+        cut = (pl.ds(r0, nr), pl.ds(c0, nc))
+        fixed = {b: 1 - bits[b]} if theirs else {}
+        part = arrays[array].at[at_bits(bits, order[:phase], fixed) + cut]
+        src = stage.at[cut] if array == 1 and phase == 0 and not theirs else part
         return pltpu.make_async_remote_copy(
-            src_ref=part, dst_ref=part, send_sem=fsend.at[u, phase], recv_sem=frecv.at[u, phase],
+            src_ref=src, dst_ref=part, send_sem=fsend.at[u, phase], recv_sem=frecv.at[u, phase],
             device_id={"fsdp": partner_of(me, bits, b)}, device_id_type=MESH_ID,
         )
 
     def landed(u, phase):
-        array, r0, nr, c0, nc, which = units[u]
-        order = order_list[which]
-        b = order[phase]
-        part = arrays[array].at[
-            at_bits(bits, order[:phase], {b: 1 - bits[b]}) + (pl.ds(r0, nr), pl.ds(c0, nc))
-        ]
-        pltpu.make_async_remote_copy(
-            src_ref=part, dst_ref=part, send_sem=fsend.at[u, phase], recv_sem=frecv.at[u, phase],
-            device_id={"fsdp": partner_of(me, bits, b)}, device_id_type=MESH_ID,
-        ).wait_recv()
+        hop(u, phase, True).wait_recv()
+
+    def onward(some, phase):
+        for u in some:
+            landed(u, phase - 1)
+            hop(u, phase).start()
+
+    def needed(side, taker, start, height):
+        low, high = key_span(taker, rows, glen)
+        if side == 0:
+            return (start < prompt) | (start + height > low)
+        return (start < prompt) | (start < high)
 
     copies[0].wait()
     copies[1].wait()
-    chains = [
-        Chain(x_all.at[0], rows, (zsend, zrecv), 0, rank, count),
-        Chain(e_all, erows, (zsend, zrecv), 1, rank, count),
-        Chain(x_all.at[1], rows, (zsend, zrecv), 2, rank, count),
-    ]
-    for chain in chains:
-        chain.start(0)
+    sems = (zsend, zrecv)
+    strips = rows // STRIP
+    toks = [Chain(x_all.at[m], rows, strips, sems, m, rank, count, needed) for m in range(MICRO)]
+    encs = Chain(e_all, erows, 1, sems, MICRO, rank, count, None)
+    toks[0].start(0)
+    encs.start(0)
     halo = pltpu.make_async_remote_copy(
         src_ref=cot.at[:, pl.ds(rows - HALO, HALO)], dst_ref=prev, send_sem=csend, recv_sem=crecv,
         device_id={"seq": rank + 1}, device_id_type=MESH_ID,
@@ -726,30 +710,105 @@
     def _():
         halo.start()
 
+    for strip in range(glen // STRIP):
+        start, block = strip * STRIP, strip * STRIP // rows
+        side0, side1 = needed(0, rank, start, STRIP), needed(1, rank, start, STRIP)
+        unseen = ((block < rank) & jnp.logical_not(side0)) | ((block > rank) & jnp.logical_not(side1))
+
+        @pl.when(unseen)
+        def _():
+            x_all[:, start : start + STRIP, :] = jnp.zeros((MICRO, STRIP, D), BF)
+
     for copy in copies[2:]:
         copy.wait()
-    for u in range(len(units)):
+    everything = list(range(len(units)))
+    for u in everything:
         hop(u, 0).start()
-    jobs = []
-    for phase in range(1, d):
-        for u in range(len(units)):
-            jobs.append((u, phase))
-    steps = [(s, c) for s in range(1, count) for c in chains]
-    share = -(-len(jobs) // max(1, len(steps)))
-    while jobs or steps:
-        for u, phase in jobs[:share]:
-            landed(u, phase - 1)
-            hop(u, phase).start()
-        jobs = jobs[share:]
-        if steps:
-            s, chain = steps.pop(0)
-            chain.arrived(s - 1)
-            if s < count - 1:
-                chain.start(s)
-    for u in range(len(units)):
+    settle = pltpu.make_async_copy(stage, wb.at[here], local.at[len(copies)])
+    settle.start()
+    first = pltpu.make_async_copy(cot.at[:, pl.ds(rows - HALO, HALO)], prev, local.at[len(copies) + 1])
+
+    @pl.when(rank == 0)
+    def _():
+        first.start()
+
+    settle.wait()
+    onward(everything[:6], 1)
+    for s in range(1, count):
+        toks[0].arrived(s - 1, s < count - 1)
+        if s == 1:
+            onward(everything[6:], 1)
+            toks[1].start(0) if count == 2 else None
+        if s == count - 2:
+            toks[1].start(0)
+        encs.arrived(s - 1, s < count - 1)
+    if d > 2:
+        for phase in range(2, d):
+            onward(everything[:2], phase)
+    landed(0, d - 1)
+    landed(1, d - 1)
+
+    off = pl.multiple_of(rank * rows, 128)
+    edge = pl.multiple_of(jnp.minimum(rank * rows + rows, glen - 128), 128)
+    n_lead = (n, 3 * piece, D)
+
+    def weight(name):
+        start, size = table_a[name]
+        return wa[(slice(None),) * d + (slice(start, start + size),)].reshape(D, D)
+
+    def project(m):
+        def one_tile(tile, _):
+            at = pl.ds(pl.multiple_of(tile * 256, 256), 256)
+            part = x_all[m, at, :]
+            k_ref[m, at, :] = nn(part, weight("wk")).astype(BF)
+            v_ref[m, at, :] = nn(part, weight("wv")).astype(BF)
+            return 0
+
+        lax.fori_loop(0, glen // 256, one_tile, 0)
+        edge_rows = x_all[m, pl.ds(edge, HALO), :]
+        halo_out[m] = edge_rows
+        q_ref[m, 0:rows, :] = (nn(x_all[m, pl.ds(off, rows), :], weight("wq")).astype(BF) * SCALE).astype(BF)
+        q_ref[m, rows : rows + HALO, :] = (nn(edge_rows, weight("wq")).astype(BF) * SCALE).astype(BF)
+        place_info(info, seg_ref, prefix_ref, m)
+        seg_row = info[1:2, :]
+        place = lax.broadcasted_iota(jnp.int32, (1, glen), 1)
+        for start, size, span in ((0, rows, pl.ds(off, rows)), (rows, HALO, pl.ds(edge, 128))):
+            column = info[:, span].T[0:size]
+            limit, seg = column[:, 0:1], column[:, 1:2]
+            seen = jnp.where(
+                place < prompt, (place.astype(F32) < limit).astype(jnp.int32), (seg_row == seg).astype(jnp.int32)
+            )
+            bias[start : start + size, :] = jnp.where(seen == 1, 0.0, NEG)
+
+    def pairs(m, low, high):
+        def one_pair(pair, _):
+            at = lanes_of(pair)
+            mix = attend_pair(
+                q_ref[m, :, at], k_ref[m, :, at], v_ref[m, :, at], bias[...], pair, lse_sc
+            )
+            mix_ref[m, :, at] = mix.astype(BF)
+            return 0
+
+        lax.fori_loop(low, high, one_pair, 0)
+        if high == HEADS // 2:
+            lse_out[m] = lse_sc[0:rows, :].T[0:HEADS, :]
+
+    rest = everything[2:]
+    project(0)
+    pairs(0, 0, 2)
+    toks[1].arrived(0, count > 2)
+    for phase in range(2, d):
+        onward(rest[: len(rest) // 2], phase)
+    pairs(0, 2, 4)
+    for s in range(2, count):
+        toks[1].arrived(s - 1, s < count - 1)
+    for phase in range(2, d):
+        onward(rest[len(rest) // 2 :], phase)
+    project(1)
+    pairs(1, 0, 4)
+
+    for u in rest:
         landed(u, d - 1)
-
-    first = pltpu.make_async_copy(cot.at[:, pl.ds(rows - HALO, HALO)], prev, local.at[len(copies)])
 
     @pl.when(rank > 0)
     def _():
@@ -757,23 +816,24 @@
 
     @pl.when(rank == 0)
     def _():
-        first.start()
         first.wait()
 
     @pl.when(rank < last)
     def _():
         halo.wait_send()
 
-    for u in range(len(units)):
+    for u in everything:
         for phase in range(d):
             hop(u, phase).wait_send()
-    for chain in chains:
+    for chain in toks + [encs]:
         for s in range(count - 1):
             chain.sent(s)
 
 
-def gather(n, count, shards, small, tok, enc, cot):
+def front(n, count, shards, small, tok, enc, cot, seg, prefix):
     rows, erows = tok.shape[1], enc.shape[1]
+    glen = count * rows
+    ext = rows + HALO
     lead = (2,) * bit_count(n)
     _, ra = qkv_rows(n)
     _, rb = rest_rows(n)
@@ -781,27 +841,36 @@
     d = bit_count(n)
     hbm = pl.BlockSpec(memory_space=pl.ANY)
     dma = pltpu.SemaphoreType.DMA
+    strips = rows // STRIP
     return pl.pallas_call(
-        functools.partial(gather_kernel, n, count, rows, erows),
-        in_specs=[hbm] * 15,
-        out_specs=[hbm] * 6,
+        functools.partial(front_kernel, n, count, rows, erows),
+        in_specs=[hbm] * 15 + [VM, SMEM],
+        out_specs=[VM, hbm] + [VM] * 10,
         out_shape=[
             jax.ShapeDtypeStruct(lead + (ra, D), BF),
             jax.ShapeDtypeStruct(lead + (rb, D), BF),
             jax.ShapeDtypeStruct(lead + (8, 128), F32),
-            jax.ShapeDtypeStruct((MICRO, count * rows, D), BF),
+            jax.ShapeDtypeStruct((MICRO, glen, D), BF),
             jax.ShapeDtypeStruct((MICRO, count * erows, D), BF),
             jax.ShapeDtypeStruct((MICRO, HALO, D), BF),
+            jax.ShapeDtypeStruct((MICRO, HALO, D), BF),
+            jax.ShapeDtypeStruct((MICRO, ext, D), BF),
+            jax.ShapeDtypeStruct((MICRO, glen, D), BF),
+            jax.ShapeDtypeStruct((MICRO, glen, D), BF),
+            jax.ShapeDtypeStruct((MICRO, ext, D), BF),
+            jax.ShapeDtypeStruct((MICRO, HEADS, rows), F32),
         ],
         scratch_shapes=[
-            dma((18,)), dma((units, d)), dma((units, d)),
-            dma((3, 2, count)), dma((3, 2, count)), dma(()), dma(()),
+            pltpu.VMEM((rb, D), BF), pltpu.VMEM((ext, glen), F32), pltpu.VMEM((ext, 128), F32),
+            pltpu.VMEM((8, glen), F32),
+            dma((20,)), dma((units, d)), dma((units, d)),
+            dma((MICRO + 1, 2, count, strips)), dma((MICRO + 1, 2, count, strips)), dma(()), dma(()),
         ],
         compiler_params=pltpu.CompilerParams(
             collective_id=0, has_side_effects=True, vmem_limit_bytes=60 * MIB
         ),
-        name="gather",
-    )(*shards, small, tok, enc, cot)
+        name="front",
+    )(*shards, small, tok, enc, cot, seg, prefix)
 
 
 def reduce_kernel(n, count, rows, erows, *refs):
@@ -1056,12 +1125,8 @@
 ):
     n = lax.axis_size("fsdp")
     count = lax.axis_size("seq")
-    rank = lax.axis_index("seq")
     tokens = tokens[:, 0]
     rows = tokens.shape[1]
-    seg = segment_ids[:, 0]
-    glen = seg.shape[1]
-    prompt = glen // 3
     prefix = prefix_len[:, 0]
     cot = cotangent[:, 0]
 
@@ -1071,44 +1136,22 @@
         [b_up, b_down, gain_one, shift_one, gain_two, shift_two, gain_three, shift_three]
     ).astype(F32)
     small = jnp.pad(small, (0, 1024 - small.shape[0])).reshape(8, 128)
-    wa, wb, small_all, x_all, e_all, previous = gather(
-        n, count, shards, small, tokens, encoded[:, 0], cot
-    )
+    (
+        wa, wb, small_all, x_all, e_all, previous, edges, q, k, v, mix, lse
+    ) = front(n, count, shards, small, tokens, encoded[:, 0], cot, segment_ids, prefix)
     wa = wa.reshape((n,) + wa.shape[-2:])
     wb = wb.reshape((n,) + wb.shape[-2:])
     small_all = small_all.reshape(n, 1024)
     bup = small_all[:, :edge].reshape(1, FF)
     vecs = small_all[:, edge : edge + 7 * side].reshape(n, 7, side).transpose(1, 0, 2).reshape(7, D)
     vecs = jnp.concatenate([vecs, jnp.zeros((1, D), F32)], axis=0)
-    shifted = jnp.concatenate([previous[:, HALO - 1 :], cot[:, : rows - 1]], axis=1)
-
-    numbers = jnp.arange(1, prefix.shape[1] + 1, dtype=jnp.int32)
-    limit = jnp.sum(
-        jnp.where(seg[:, :, None] == numbers[None, None, :], prefix[:, None, :], 0), axis=2
+
+    slot_out, dmix, dr1, genc, gb, g_bup, g_vec = middle(
+        mix, tokens, edges, e_all, cot, previous, segment_ids, prefix, wb, bup, vecs, rows
     )
-    limit = jnp.where(seg == 0, prompt, limit)
-    col = jnp.stack([limit, seg], axis=2)
-    row = jnp.stack([limit, seg], axis=1)
-    same = jnp.concatenate(
-        [jnp.zeros((MICRO, 1), F32), (seg[:, 1:] == seg[:, :-1]).astype(F32), jnp.zeros((MICRO, 1), F32)],
-        axis=1,
+    own, part, ga = self_backward(
+        x_all, q, k, v, mix, dmix, dr1, lse, segment_ids, prefix, wa, rows
     )
-    offset = rank * rows
-    flags = jnp.stack(
-        [
-            lax.dynamic_slice_in_dim(same, offset + 1, rows, 1),
-            lax.dynamic_slice_in_dim(same, offset, rows, 1),
-        ],
-        axis=2,
-    )
-    start = jnp.minimum(offset + rows, glen - HALO)
-    x_ext = jnp.concatenate([tokens, lax.dynamic_slice_in_dim(x_all, start, HALO, 1)], axis=1)
-
-    q, k, v, mix, lse = self_forward(x_all, wa, col, row[:, 1:2], rows)
-    slot_out, dmix, dr1, genc, gb, g_bup, g_vec = middle(
-        mix, x_ext, e_all, cot, shifted, flags, wb, bup, vecs, rows
-    )
-    own, part, ga = self_backward(x_all, q, k, v, mix, dmix, dr1, lse, row, wa, rows)
 
     gs = jnp.concatenate(
         [

time: 477 us -> 412 us (0.86)
  Pallas kernels: 453 us -> 392 us
  other arithmetic: 6.69 us -> 0.61 us
    pallas_call x2 -> x1, Pallas kernels: 152 us -> 66.6 us  [front(): pl.pallas_call(functools.partial(front_kernel, n, count, rows, erows), in...]
    pallas_call x1, Pallas kernels: 189 us -> 214 us  [reduce_out(): pl.pallas_call(functools.partial(reduce_kernel, n, count, rows, erows), i...]
    concatenate x1, local copies, waits for them, and re-layouts: 0.09 us -> 5.41 us  [on_device(): jnp.concatenate([b_up, b_down, gain_one, shift_one, gain_two, shift_two,...]
where the time goes in v3:
time: 412 us; the launch traced here: 411 us
  Pallas kernels  392 us (95%)
  local copies, waits for them, and re-layouts  17.8 us (4%)
    pallas_call x1, Pallas kernels, reduce_out(): pl.pallas_call(functools.partial(reduce_kernel, n, count, rows, erows), i...  214 us
    pallas_call x1, Pallas kernels, front(): pl.pallas_call(functools.partial(front_kernel, n, count, rows, erows), in...  66.6 us
    pallas_call x1, Pallas kernels, self_backward(): pl.pallas_call(functools.partial(self_backward_kernel, glen, rows), in_sp...  64.9 us
    pallas_call x1, Pallas kernels, middle(): pl.pallas_call(functools.partial(middle_kernel, rows, enc), in_specs=[VM]...  47.1 us

profile of v3, /device:TPU:0, one launch (start us, length us, event | category | flops | bytes accessed | tf_op | source)
XLA Modules:
  0.0 411.4 jit_solution(14177916955523102361)
XLA Ops:
  0.7 5.4 %concatenate.9 = bf16[704]{0:T(1024)(128)(2,1)S(1)} concatenate(bf16[256]{0:T(256)(128)(2,1)} %param.38, bf16[64]{0:T(256)(128)(2,1)} %param.40, bf16[64]{0:T(256)(128)(2,1)} %param.41, bf16[64]{0:T(256)(128)(2,1)} %param.42, bf16[64]{0:T(256)(128)(2,1)} %param.43, bf16[64]{0:T(256)(128)(2,1)} %param.44, bf16[64]{0:T(256)(128)(2,1)} %param.45, bf16[64]{0:T(256)(128)(2,1)} %param.46), dimensions={0} | concatenate | bytes 2816 | tf_op jit(solution)/shard_map/concatenate | solution.py:1135
  6.1 0.6 bitcast_convert_fusion.refs_11_
  6.7 66.6 %front.1 = (bf16[2,2,2,192,512]{4,3,2,1,0:T(8,128)(2,1)}, bf16[2,2,2,960,512]{4,3,2,1,0:T(8,128)(2,1)}, f32[2,2,2,8,128]{4,3,2,1,0:T(8,128)}, bf16[2,1536,512]{2...) custom-call(bf16[64,512]{1,0:T(8,128)(2,1)} %refs_0_.1, ...), custom_call_target="tpu_custom_call" | custom-call | tf_op jit(solution)/shard_map/front/pallas_call | solution.py:845
  73.3 0.8 copy.63
  74.0 0.1 reshape.100
  74.1 0.1 reshape.101
  74.2 0.6 concatenate.10.vec_ref
  74.8 0.6 copy.59
  75.4 47.1 %middle.1 = (bf16[2,384,512]{2,1,0:T(8,128)(2,1)}, bf16[2,384,512]{2,1,0:T(8,128)(2,1)}, f32[2,384,512]{2,1,0:T(8,128)}, bf16[2,256,512]{2,1,0:T(8,128)(2,1)}, b...) custom-call(bf16[2,400,512]{2,1,0:T(8,128)(2,1)} %get-tuple-element.49.mix_ref, ...), custom_call_target="tpu_custom_call" | custom-call | tf_op jit(solution)/shard_map/middle/pallas_call | solution.py:403
  122.6 0.8 reshape.106
  123.4 0.1 reshape.107
  123.4 0.9 slice_reduce_fusion
  124.3 0.1 pad.9.clone
  124.4 0.6 copy.60
  125.0 64.9 %self_backward.1 = (f32[2,384,512]{2,1,0:T(8,128)}, bf16[2,1536,512]{2,1,0:T(8,128)(2,1)}, bf16[8,192,512]{2,1,0:T(8,128)(2,1)}) custom-call(bf16[2,1536,512]{2,1,0:T(8,128)(2,1)} %get-tuple-element.56.x_ref, bf16[2,400,512]{2,1,0:T(8,128)(2,1)} %get-tuple-element.57.q_ref, bf16[2,1536,512]{2,1,0:T(8,128)(2,1)} %get-tuple-element.58.k_ref, ...), custom_call_target="tpu_custom_call" | custom-call | tf_op jit(solution)/shard_map/self_backward/pallas_call | solution.py:504
  189.9 213.6 %reduce_out.1 = (f32[192,512]{1,0:T(8,128)}, f32[960,512]{1,0:T(8,128)}, f32[8,128]{1,0:T(8,128)}, f32[2,384,512]{2,1,0:T(8,128)}, f32[2,64,512]{2,1,0:T(8,128)}) custom-call(bf16[2,2,2,192,512]{4,3,2,1,0:T(8,128)(2,1)} %bitcast.53, bf16[2,2,2,960,512]{4,3,2,1,0:T(8,128)(2,1)} %bitcast.46, f32[2,2,2,8,128]{4,3,2,1,0:T(8,128)} %bitcast.58, ...), custom_call_target="tpu_custom_call" | custom-call | tf_op jit(solution)/shard_map/reduce_out/pallas_call | solution.py:1106
  403.5 2.4 fusion.1
  405.9 0.9 fusion
  406.8 0.8 copy.57
  407.6 0.7 slice.95
  408.3 0.6 fusion.3
  408.9 0.6 slice_bitcast_fusion.1
  409.5 1.1 copy.67
  410.7 0.7 copy.68
  (15 shorter events, 0.1 us)
Async XLA Ops:
  403.5 2.4 copy-start
  405.9 2.4 copy-start.3
  405.9 3.6 copy-start.1
  407.6 3.0 copy-start.2
